TPU v7x, 32 devices: a whole 2x2x4 slice. The times are simulated.
32 devices in a mesh: rows: 4 (over z), fsdp: 8 (over y, x, core).
Axes of the slice: x: 2, y: 2, z: 4, core: 2. Of those that a mesh axis runs over, the one named last changes fastest.
Arguments:
- tokens: bfloat16 [32, 512, 1024], P(('rows', 'fsdp')), may hold values from -6 to 6
- time_embed: bfloat16 [32, 256], P(('rows', 'fsdp')), may hold values from -6 to 6
- segment_ids: int32 [32, 512], P(('rows', 'fsdp')), may hold values from 0 to 3, never falling along the last dimension, each value on 1 to 256 neighbouring positions
- cotangent: bfloat16 [32, 512, 1024], P(('rows', 'fsdp')), may hold values from -6 to 6
- mixing_w: float32 [4, 1024, 1024], P(None, 'fsdp'), may hold values from -0.25 to 0.25
- mixing_m: float32 [4, 1024, 1024], P(None, 'fsdp'), may hold values from -384 to 384
- mixing_v: float32 [4, 1024, 1024], P(None, 'fsdp'), may hold values from 4096 to 16384
- mixing_avg: float32 [4, 1024, 1024], P(None, 'fsdp'), may hold values from -0.25 to 0.25
- cond_w: float32 [2, 256, 1024], P(None, 'fsdp'), may hold values from -0.1875 to 0.1875
- cond_m: float32 [2, 256, 1024], P(None, 'fsdp'), may hold values from -768 to 768
- cond_v: float32 [2, 256, 1024], P(None, 'fsdp'), may hold values from 16384 to 65536
- cond_avg: float32 [2, 256, 1024], P(None, 'fsdp'), may hold values from -0.1875 to 0.1875
- up_w: float32 [1024, 4096], P('fsdp'), may hold values from -0.1875 to 0.1875
- up_m: float32 [1024, 4096], P('fsdp'), may hold values from -224 to 224
- up_v: float32 [1024, 4096], P('fsdp'), may hold values from 1489 to 5957
- up_avg: float32 [1024, 4096], P('fsdp'), may hold values from -0.1875 to 0.1875
- down_w: float32 [4096, 1024], P('fsdp'), may hold values from -0.09375 to 0.09375
- down_m: float32 [4096, 1024], P('fsdp'), may hold values from -448 to 448
- down_v: float32 [4096, 1024], P('fsdp'), may hold values from 5898 to 23592
- down_avg: float32 [4096, 1024], P('fsdp'), may hold values from -0.09375 to 0.09375
Outputs:
- output: bfloat16 [32, 512, 1024], P(('rows', 'fsdp'))
- input_grad: bfloat16 [32, 512, 1024], P(('rows', 'fsdp'))
- mixing_grad: float32 [4, 1024, 1024], P(None, 'fsdp')
- mixing_m_out: float32 [4, 1024, 1024], P(None, 'fsdp')
- mixing_v_out: float32 [4, 1024, 1024], P(None, 'fsdp')
- mixing_w_out: float32 [4, 1024, 1024], P(None, 'fsdp')
- mixing_avg_out: float32 [4, 1024, 1024], P(None, 'fsdp')
- cond_grad: float32 [2, 256, 1024], P(None, 'fsdp')
- cond_m_out: float32 [2, 256, 1024], P(None, 'fsdp')
- cond_v_out: float32 [2, 256, 1024], P(None, 'fsdp')
- cond_w_out: float32 [2, 256, 1024], P(None, 'fsdp')
- cond_avg_out: float32 [2, 256, 1024], P(None, 'fsdp')
- up_grad: float32 [1024, 4096], P('fsdp')
- up_m_out: float32 [1024, 4096], P('fsdp')
- up_v_out: float32 [1024, 4096], P('fsdp')
- up_w_out: float32 [1024, 4096], P('fsdp')
- up_avg_out: float32 [1024, 4096], P('fsdp')
- down_grad: float32 [4096, 1024], P('fsdp')
- down_m_out: float32 [4096, 1024], P('fsdp')
- down_v_out: float32 [4096, 1024], P('fsdp')
- down_w_out: float32 [4096, 1024], P('fsdp')
- down_avg_out: float32 [4096, 1024], P('fsdp')
Inputs may be any that keep to these rules, and one draw needn't show every extreme that they name: `segment_ids`: ids never fall along a row; a row has at most 4 segments, each of 1 to 256 tokens, and one segment of a row has exactly 256.
All inputs are finite; a program needn't handle non-finite values.
Results may differ from a plain program's by a relative error of at most 0.023.
The roundings to bfloat16 on the way count: a program that leaves them out, or rounds other values in their place, can miss the bound.
Values may be sent and summed in bfloat16 or wider, within the bound.
A program may use at most 320 MiB of HBM per device.

v0:
```python
import jax
import jax.numpy as jnp
from jax import lax
from jax.sharding import PartitionSpec as P

D = 1024
HEADS = 16
HEAD_DIM = 64
STEP = 7


def normed(values):
    center = values - jnp.mean(values, axis=-1, keepdims=True)
    spread = jnp.mean(center * center, axis=-1, keepdims=True)
    return center * lax.rsqrt(spread + 1e-05)


def scaled_norm(values, gain):
    return normed(values) * gain[None, :]


def rotary_tables(segments):
    length = segments.shape[0]
    position = jnp.arange(length, dtype=jnp.int32)
    is_start = jnp.concatenate([jnp.ones((1,), dtype=bool), segments[1:] != segments[:-1]])
    seg_start = lax.cummax(jnp.where(is_start, position, jnp.zeros_like(position)), axis=0)
    offset = (position - seg_start).astype(jnp.float32)
    frequency = 10000.0 ** (-jnp.arange(HEAD_DIM // 2, dtype=jnp.float32) * 2.0 / HEAD_DIM)
    turned = offset[:, None] * frequency[None, :]
    return (jnp.cos(turned)[:, None, :], jnp.sin(turned)[:, None, :])


def rotate(parts, cos_table, sin_table):
    half_dim = parts.shape[-1] // 2
    part_a = parts[..., :half_dim]
    part_b = parts[..., half_dim:]
    return jnp.concatenate(
        [part_a * cos_table - part_b * sin_table, part_b * cos_table + part_a * sin_table], axis=-1
    )


def unrotate(grads, cos_table, sin_table):
    half_dim = grads.shape[-1] // 2
    grad_a = grads[..., :half_dim]
    grad_b = grads[..., half_dim:]
    return jnp.concatenate(
        [grad_a * cos_table + grad_b * sin_table, grad_b * cos_table - grad_a * sin_table], axis=-1
    )


def adam_update(gradient, weight, moment_one, moment_two, average):
    moment_one_new = 0.5 * moment_one + 0.5 * gradient
    moment_two_new = 0.5 * moment_two + 0.5 * gradient * gradient
    correction = 1.0 - 0.5**STEP
    update = (
        moment_one_new / correction / (jnp.sqrt(moment_two_new / correction) + 1e-08) + 0.1 * weight
    )
    weight_new = weight - 0.01 * update
    average_new = 0.8 * average + 0.2 * weight_new
    return (moment_one_new, moment_two_new, weight_new, average_new)


def local(
    tokens,
    time_embed,
    segment_ids,
    cotangent,
    mixing_w,
    mixing_m,
    mixing_v,
    mixing_avg,
    cond_w,
    cond_m,
    cond_v,
    cond_avg,
    up_w,
    up_m,
    up_v,
    up_avg,
    down_w,
    down_m,
    down_v,
    down_avg,
):
    rows_in = tokens[0].astype(jnp.float32)
    embedding = time_embed[0]
    segments = segment_ids[0]
    length = rows_in.shape[0]
    block_rows = min(512, length)
    block_count = length // block_rows
    mixing_g, cond_g = (
        lax.all_gather(mixing_w.astype(jnp.bfloat16), "fsdp", axis=1, tiled=True),
        lax.all_gather(cond_w.astype(jnp.bfloat16), "fsdp", axis=1, tiled=True),
    )
    up_g, down_g = (
        lax.all_gather(up_w.astype(jnp.bfloat16), "fsdp", axis=0, tiled=True),
        lax.all_gather(down_w.astype(jnp.bfloat16), "fsdp", axis=0, tiled=True),
    )
    scales = 1.0 + jnp.einsum("e,ked->kd", embedding, cond_g, preferred_element_type=jnp.float32)
    cos_table, sin_table = rotary_tables(segments)
    normed_one = (normed(rows_in) * scales[0][None, :]).astype(jnp.bfloat16)
    projected = jnp.einsum(
        "td,kde->kte", normed_one, mixing_g[:3], preferred_element_type=jnp.float32
    )
    queries = rotate(projected[0].reshape(length, HEADS, HEAD_DIM), cos_table, sin_table).astype(
        jnp.bfloat16
    )
    keys_rot = rotate(projected[1].reshape(length, HEADS, HEAD_DIM), cos_table, sin_table).astype(
        jnp.bfloat16
    )
    values_b = projected[2].astype(jnp.bfloat16).reshape(length, HEADS, HEAD_DIM)
    query_blocks = queries.reshape(block_count, block_rows, HEADS, HEAD_DIM)
    seg_blocks = segments.reshape(block_count, block_rows)

    def block_scores(q_block, seg_block):
        raw = (
            jnp.einsum("qhd,khd->hqk", q_block, keys_rot, preferred_element_type=jnp.float32)
            * 0.125
        )
        same_seg = seg_block[:, None] == segments[None, :]
        return jnp.where(same_seg[None], raw, -1e30)

    def attend_block(element):
        q_block, seg_block = element
        raw = block_scores(q_block, seg_block)
        peak = jnp.max(raw, axis=-1, keepdims=True)
        exp_scores = jnp.exp(raw - peak)
        totals = jnp.sum(exp_scores, axis=-1, keepdims=True)
        probs = (exp_scores / totals).astype(jnp.bfloat16)
        out_block = jnp.einsum(
            "hqk,khd->qhd", probs, values_b, preferred_element_type=jnp.float32
        ).astype(jnp.bfloat16)
        return (out_block, peak[..., 0] + jnp.log(totals[..., 0]))

    attended, log_totals = lax.map(attend_block, (query_blocks, seg_blocks))
    attended = attended.reshape(length, D)
    middle = rows_in + jnp.dot(attended, mixing_g[3], preferred_element_type=jnp.float32)
    normed_two = (normed(middle) * scales[1][None, :]).astype(jnp.bfloat16)
    hidden_pre = jnp.dot(normed_two, up_g, preferred_element_type=jnp.float32)
    hidden_act = jax.nn.gelu(hidden_pre).astype(jnp.bfloat16)
    output = (middle + jnp.dot(hidden_act, down_g, preferred_element_type=jnp.float32)).astype(
        jnp.bfloat16
    )
    mixing_b, cond_b = (
        lax.all_gather(mixing_w.astype(jnp.bfloat16), "fsdp", axis=1, tiled=True),
        lax.all_gather(cond_w.astype(jnp.bfloat16), "fsdp", axis=1, tiled=True),
    )
    up_b, down_b = (
        lax.all_gather(up_w.astype(jnp.bfloat16), "fsdp", axis=0, tiled=True),
        lax.all_gather(down_w.astype(jnp.bfloat16), "fsdp", axis=0, tiled=True),
    )
    back_out = cotangent[0]
    d_act = jnp.einsum("td,fd->tf", back_out, down_b, preferred_element_type=jnp.float32)
    d_down = jnp.einsum("tf,td->fd", hidden_act, back_out, preferred_element_type=jnp.float32)
    _, gelu_pull = jax.vjp(jax.nn.gelu, hidden_pre)
    d_pre = gelu_pull(d_act)[0].astype(jnp.bfloat16)
    d_up = jnp.einsum("td,tf->df", normed_two, d_pre, preferred_element_type=jnp.float32)
    d_normed_two = jnp.einsum("tf,df->td", d_pre, up_b, preferred_element_type=jnp.float32)
    _, norm_pull_two = jax.vjp(scaled_norm, middle, scales[1])
    d_middle, d_scale_two = norm_pull_two(d_normed_two)
    d_middle = d_middle + back_out.astype(jnp.float32)
    d_middle_b = d_middle.astype(jnp.bfloat16)
    d_out_proj = jnp.einsum("td,te->de", attended, d_middle_b, preferred_element_type=jnp.float32)
    d_attended = jnp.einsum(
        "te,de->td", d_middle_b, mixing_b[3], preferred_element_type=jnp.float32
    ).astype(jnp.bfloat16)
    d_att_blocks = d_attended.reshape(block_count, block_rows, HEADS, HEAD_DIM)

    def back_block(state_in, element):
        q_block, seg_block, d_block, log_block = element
        raw = block_scores(q_block, seg_block)
        probs_f = jnp.exp(raw - log_block[..., None])
        probs_b = probs_f.astype(jnp.bfloat16)
        d_probs = jnp.einsum("qhd,khd->hqk", d_block, values_b, preferred_element_type=jnp.float32)
        d_raw = (probs_f * (d_probs - jnp.sum(probs_f * d_probs, axis=-1, keepdims=True))).astype(
            jnp.bfloat16
        )
        d_query = (
            jnp.einsum("hqk,khd->qhd", d_raw, keys_rot, preferred_element_type=jnp.float32) * 0.125
        )
        keys_acc = (
            state_in[0]
            + jnp.einsum("hqk,qhd->khd", d_raw, q_block, preferred_element_type=jnp.float32) * 0.125
        )
        values_acc = state_in[1] + jnp.einsum(
            "hqk,qhd->khd", probs_b, d_block, preferred_element_type=jnp.float32
        )
        return ((keys_acc, values_acc), d_query)

    zero_heads = jnp.zeros((length, HEADS, HEAD_DIM), jnp.float32)
    (d_keys, d_values), d_queries = lax.scan(
        back_block, (zero_heads, zero_heads), (query_blocks, seg_blocks, d_att_blocks, log_totals)
    )
    d_queries = unrotate(d_queries.reshape(length, HEADS, HEAD_DIM), cos_table, sin_table)
    d_keys = unrotate(d_keys, cos_table, sin_table)
    d_projected = (
        jnp.stack([d_queries, d_keys, d_values]).reshape(3, length, D).astype(jnp.bfloat16)
    )
    d_qkv = jnp.einsum("td,kte->kde", normed_one, d_projected, preferred_element_type=jnp.float32)
    d_normed_one = jnp.einsum(
        "kte,kde->td", d_projected, mixing_b[:3], preferred_element_type=jnp.float32
    )
    _, norm_pull_one = jax.vjp(scaled_norm, rows_in, scales[0])
    d_rows, d_scale_one = norm_pull_one(d_normed_one)
    input_grad = (d_middle + d_rows).astype(jnp.bfloat16)
    d_scales = jnp.stack([d_scale_one, d_scale_two])
    d_cond = embedding.astype(jnp.float32)[None, :, None] * d_scales[:, None, :]
    d_mixing = jnp.concatenate([d_qkv, d_out_proj[None]], axis=0)
    mixing_part, cond_part = (
        lax.psum_scatter(d_mixing, "fsdp", scatter_dimension=1, tiled=True),
        lax.psum_scatter(d_cond, "fsdp", scatter_dimension=1, tiled=True),
    )
    up_part, down_part = (
        lax.psum_scatter(d_up, "fsdp", scatter_dimension=0, tiled=True),
        lax.psum_scatter(d_down, "fsdp", scatter_dimension=0, tiled=True),
    )
    mixing_grad, cond_grad, up_grad, down_grad = (
        lax.psum(mixing_part.astype(jnp.bfloat16), "rows").astype(jnp.float32),
        lax.psum(cond_part.astype(jnp.bfloat16), "rows").astype(jnp.float32),
        lax.psum(up_part.astype(jnp.bfloat16), "rows").astype(jnp.float32),
        lax.psum(down_part.astype(jnp.bfloat16), "rows").astype(jnp.float32),
    )
    mix_one, mix_two, mix_new, mix_average = adam_update(
        mixing_grad, mixing_w, mixing_m, mixing_v, mixing_avg
    )
    cond_one, cond_two, cond_new, cond_average = adam_update(
        cond_grad, cond_w, cond_m, cond_v, cond_avg
    )
    up_one, up_two, up_new, up_average = adam_update(up_grad, up_w, up_m, up_v, up_avg)
    down_one, down_two, down_new, down_average = adam_update(
        down_grad, down_w, down_m, down_v, down_avg
    )
    return (
        output[None],
        input_grad[None],
        mixing_grad,
        mix_one,
        mix_two,
        mix_new,
        mix_average,
        cond_grad,
        cond_one,
        cond_two,
        cond_new,
        cond_average,
        up_grad,
        up_one,
        up_two,
        up_new,
        up_average,
        down_grad,
        down_one,
        down_two,
        down_new,
        down_average,
    )


def solution(mesh):
    placed = (
        P(("rows", "fsdp"), None, None),
        P(("rows", "fsdp"), None),
        P(("rows", "fsdp"), None),
        P(("rows", "fsdp"), None, None),
        P(None, "fsdp", None),
        P(None, "fsdp", None),
        P(None, "fsdp", None),
        P(None, "fsdp", None),
        P(None, "fsdp", None),
        P(None, "fsdp", None),
        P(None, "fsdp", None),
        P(None, "fsdp", None),
        P("fsdp", None),
        P("fsdp", None),
        P("fsdp", None),
        P("fsdp", None),
        P("fsdp", None),
        P("fsdp", None),
        P("fsdp", None),
        P("fsdp", None),
    )
    return jax.shard_map(
        local,
        mesh=mesh,
        in_specs=placed,
        out_specs=(
            P(("rows", "fsdp"), None, None),
            P(("rows", "fsdp"), None, None),
            P(None, "fsdp", None),
            P(None, "fsdp", None),
            P(None, "fsdp", None),
            P(None, "fsdp", None),
            P(None, "fsdp", None),
            P(None, "fsdp", None),
            P(None, "fsdp", None),
            P(None, "fsdp", None),
            P(None, "fsdp", None),
            P(None, "fsdp", None),
            P("fsdp", None),
            P("fsdp", None),
            P("fsdp", None),
            P("fsdp", None),
            P("fsdp", None),
            P("fsdp", None),
            P("fsdp", None),
            P("fsdp", None),
            P("fsdp", None),
            P("fsdp", None),
        ),
        check_vma=False,
    )
```

profile of v0, /device:TPU:0, one launch (start us, length us, event | category | flops | bytes accessed | tf_op | source)
XLA Modules:
  0.0 871.2 jit_solution(4540163234994923298)
XLA Ops:
  8.9 2.9 convert_element_type.117
  13.1 2.8 convert_element_type.126
  18.6 18.1 %all-gather.5.cloned.1.call-done = bf16[2,256,1024]{2,1,0:T(8,128)(2,1)} async-done(((bf16[2,32,1024]{2,1,0:T(8,128)(2,1)}), bf16[2,256,1024]{2,1,0:T(8,128)(2,1)}) %all-gather.5.cloned.1.call-update) | async-done | bytes 1048592 | tf_op jit(solution)/shard_map/all_gather | solution.py:93
  38.2 55.4 %all-gather.7.cloned.1.call-done = bf16[4,1024,1024]{2,1,0:T(8,128)(2,1)} async-done(((bf16[4,128,1024]{2,1,0:T(8,128)(2,1)}), bf16[4,1024,1024]{2,1,0:T(8,128)(2,1)}) %all-gather.7.cloned.1.call-update) | async-done | bytes 8388624 | tf_op jit(solution)/shard_map/all_gather | solution.py:92
  93.6 5.8 fusion.17
  99.5 2.7 copy-done.15
  103.6 5.2 fusion.73
  110.8 2.9 copy.71
  115.9 7.3 fusion.75
  123.3 9.6 %fusion = f32[16,512]{1,0:T(8,128)S(1)} fusion(f32[16,512,512]{1,2,0:T(8,128)} %get-tuple-element.165, f32[16,512]{1,0:T(8,128)S(1)} %get-tuple-element.164), kind=kLoop, calls=%fused_computation.7 | loop fusion | flops 8380416 | bytes 16842752 | tf_op jit(solution)/shard_map/while/body/eval_jaxpr/reduce_sum | solution.py:128
  132.9 7.6 fusion.37
  140.4 3.3 fusion.76
  144.2 6.3 all-gather.9.cloned.1.call-done
  150.5 10.6 %fusion.67 = f32[512,4096]{1,0:T(8,128)} fusion(bf16[1024,4096]{1,0:T(8,128)(2,1)} %all-gather.9.cloned.1.call-done, f32[512,1024]{1,0:T(8,128)S(1)} %get-tuple-element.167, f32[1024]{0:T(1024)S(1)} %bitcast.147, f32[512]{0:T(512)S(1)} %fusion.55, f32[512]{0:T(512)S(1)} %broadcast_multiply_fusion.1), kind=kOutput, calls=%fused_computation.136 | convolution fusion | flops 4297064448 | bytes 18882560 | tf_op jit(solution)/shard_map/dot_general | solution.py:139
  161.1 46.1 %all-gather.11.cloned.1.call-done = bf16[4096,1024]{1,0:T(8,128)(2,1)} async-done(((bf16[512,1024]{1,0:T(8,128)(2,1)}), bf16[4096,1024]{1,0:T(8,128)(2,1)}) %all-gather.11.cloned.1.call-update) | async-done | bytes 8388624 | tf_op jit(solution)/shard_map/all_gather | solution.py:97
  207.3 12.8 %fusion.8 = bf16[512,4096]{1,0:T(8,128)(2,1)S(1)} fusion(f32[512,4096]{1,0:T(8,128)} %fusion.67, bf16[4096,1024]{1,0:T(8,128)(2,1)} %all-gather.11.cloned.1.call-done, bf16[1,512,1024]{2,1,0:T(8,128)(2,1)} %param.23), kind=kOutput, calls=%fused_computation.17 | convolution fusion | flops 4336910336 | bytes 22020096 | tf_op jit(solution)/shard_map/td,fd->tf/dot_general | solution.py:153
  220.1 5.4 multiply_reduce_fusion.1
  227.6 3.3 fusion.38
  232.2 9.9 %fusion.39 = bf16[16,64,512]{2,1,0:T(8,128)(2,1)} fusion(bf16[512,16,64]{0,2,1:T(8,128)(2,1)} %bitcast.17, f32[16,512,512]{1,2,0:T(8,128)} %get-tuple-element.165, f32[16,512]{1,0:T(8,128)S(1)} %log_add_fusion), kind=kOutput, calls=%fused_computation.77 | convolution fusion | flops 545783808 | bytes 18907136 | tf_op jit(solution)/shard_map/while/body/eval_jaxpr/hqk,qhd->khd/dot_general | solution.py:185
  242.1 14.6 %multiply_reduce_fusion = (f32[16,512]{1,0:T(8,128)}, f32[16,512,512]{1,2,0:T(8,128)}) fusion(f32[16,512,512]{1,2,0:T(8,128)} %get-tuple-element.165, f32[16,512]{1,0:T(8,128)} %copy-done.43, bf16[512,16,64]{0,2,1:T(8,128)(2,1)} %bitcast.17, bf16[512,16,64]{0,2,1:T(8,128)(2,1)} %bitcast.135), kind=kOutput, calls=%fused_computation.2 | convolution fusion | flops 549445632 | bytes 35717120 | tf_op jit(solution)/shard_map/while/body/eval_jaxpr/qhd,khd->hqk/dot_general | solution.py:174
  256.8 8.2 multiply_convert_fusion
  265.0 3.2 copy-done
  269.7 7.3 multiply_bitcast_fusion
  277.0 2.3 copy.79
  284.3 7.0 fusion.31
  295.5 3.0 convolution_bitcast_fusion.1
  298.5 3.7 convolution_bitcast_fusion
  302.3 6.5 pad_maximum_fusion
  310.4 10.5 %fusion.66 = f32[1024,4096]{1,0:T(8,128)} fusion(bf16[512,4096]{1,0:T(8,128)(2,1)} %copy-done.61, f32[512,1024]{1,0:T(8,128)S(1)} %copy-done.13, f32[1024]{0:T(1024)S(1)} %bitcast.150, f32[512]{0:T(512)S(1)} %copy-done.55, f32[512]{0:T(512)S(1)} %copy-done.51), kind=kOutput, calls=%fused_computation.135 | convolution fusion | flops 4297064448 | bytes 23076864 | tf_op jit(solution)/shard_map/td,tf->df/dot_general | solution.py:157
  322.1 15.1 %fusion.46 = f32[4096,1024]{1,0:T(8,128)} fusion(bf16[1,512,1024]{2,1,0:T(8,128)(2,1)S(1)} %copy-done.19, f32[512,4096]{1,0:T(8,128)} %fusion.67), kind=kOutput, calls=%fused_computation.86 | convolution fusion | flops 4313841664 | bytes 26214400 | tf_op jit(solution)/shard_map/tf,td->fd/dot_general | solution.py:154
  339.3 117.2 %reduce-scatter.5.cloned.1.call-done = f32[4,128,1024]{1,2,0:T(8,128)} async-done(((f32[4,1024,1024]{1,2,0:T(8,128)}), f32[4,128,1024]{1,2,0:T(8,128)}) %reduce-scatter.5.cloned.1.call-update) | async-done | bytes 2097168 | tf_op jit(solution)/shard_map/reduce_scatter | solution.py:210
  456.5 2.7 convert_element_type.135
  459.2 117.3 %reduce-scatter.9.cloned.1.call-done = f32[128,4096]{1,0:T(8,128)} async-done(((f32[1024,4096]{1,0:T(8,128)}), f32[128,4096]{1,0:T(8,128)}) %reduce-scatter.9.cloned.1.call-update) | async-done | bytes 2097168 | tf_op jit(solution)/shard_map/reduce_scatter | solution.py:214
  576.5 2.7 convert_element_type.140
  579.2 117.3 %reduce-scatter.11.cloned.1.call-done = f32[512,1024]{1,0:T(8,128)} async-done(((f32[4096,1024]{1,0:T(8,128)}), f32[512,1024]{1,0:T(8,128)}) %reduce-scatter.11.cloned.1.call-update) | async-done | bytes 2097168 | tf_op jit(solution)/shard_map/reduce_scatter | solution.py:215
  696.5 2.7 convert_element_type.142
  702.6 3.0 copy.86
  707.4 3.0 copy.82
  710.5 3.4 fusion.44
  713.8 12.0 %fusion.42 = bf16[1,512,1024]{2,1,0:T(8,128)(2,1)} fusion(f32[512,1024]{1,0:T(8,128)S(1)} %copy-done.14, bf16[4096,1024]{1,0:T(8,128)(2,1)} %all-gather.11.cloned.1.call-done, f32[512,4096]{1,0:T(8,128)} %fusion.67), kind=kOutput, calls=%fused_computation.78 | convolution fusion | flops 4314890240 | bytes 19922944 | tf_op jit(solution)/shard_map/dot_general | solution.py:141
  725.8 101.5 %all-reduce.3.cloned.1.call-done = (bf16[4,128,1024]{1,2,0:T(8,128)(2,1)}, bf16[2,32,1024]{2,1,0:T(8,128)(2,1)}, bf16[128,4096]{1,0:T(8,128)(2,1)}, bf16[512,1024]{1,0:T(8,128)(2,1)}) async-done(((bf16[4,128,1024]{1,2,0:T(8,128)(2,1)}, bf16[2,32,1024]{2,1,0:T(8,128)(2,1)}, bf16[128,4096]{1,0:T(8,128)(2,1)}, bf16[512,1024]{1,0:T(8,128)(2,1)}), (bf16[4,128,1024]{1,2,0:T(8,128)(2,1)}, ...) | async-done | bytes 3276816 | tf_op jit(solution)/shard_map/psum | solution.py:218
  827.4 2.7 copy.87
  830.0 7.4 multiply_add_fusion.5
  837.4 3.0 copy.88
  842.2 3.0 copy.90
  847.3 2.4 multiply_add_fusion.7
  849.7 8.8 %multiply_add_fusion.4 = (f32[128,4096]{1,0:T(8,128)}, f32[128,4096]{1,0:T(8,128)}, f32[128,4096]{1,0:T(8,128)}, f32[128,4096]{1,0:T(8,128)}, f32[128,4096]{1,0:T(8,128)}) fusion(f32[128,4096]{1,0:T(8,128)} %param.35, f32[128,4096]{1,0:T(8,128)S(1)} %copy-done.5, f32[128,4096]{1,0:T(8,128)} %param.34, f32[128,4096]{1,0:T(8,128)} %param.33, ...), kind=kLoop, calls=%fused_computation.60 | loop fusion | flops 9437184 | bytes 19922944 | tf_op jit(solution)/shard_map/add | solution.py:59
  858.6 5.9 multiply_add_fusion.3
  (199 shorter events, 40.9 us)
Async XLA Ops:
  7.2 29.5 %all-gather.5.cloned.1.call-start = ((), (), s32[]{:S(2)}) async-start(), calls=%async_computation.4 | async-start | bytes 1179648 | tf_op jit(solution)/shard_map/all_gather | solution.py:93
  8.9 84.7 %all-gather.7.cloned.1.call-start = ((), (), s32[]{:S(2)}) async-start(), calls=%async_computation.5 | async-start | bytes 9437184 | tf_op jit(solution)/shard_map/all_gather | solution.py:92
  11.8 138.7 %all-gather.9.cloned.1.call-start = ((), (), s32[]{:S(2)}) async-start(), calls=%async_computation.6 | async-start | bytes 9437184 | tf_op jit(solution)/shard_map/all_gather | solution.py:96
  13.0 3.6 copy-start.56
  13.0 4.2 copy-start.3
  13.1 194.2 %all-gather.11.cloned.1.call-start = ((), (), s32[]{:S(2)}) async-start(), calls=%async_computation.7 | async-start | bytes 9437184 | tf_op jit(solution)/shard_map/all_gather | solution.py:97
  15.9 321.7 %reduce-scatter.7.cloned.1.call-start = ((), (), s32[]{:S(2)}) async-start(), calls=%async_computation.9 | async-start | bytes 2359296 | tf_op jit(solution)/shard_map/reduce_scatter | solution.py:211
  17.9 20.3 %copy-start.48 = (f32[512]{0:T(512)}, f32[512]{0:T(512)S(1)}, u32[]{:S(2)}) copy-start(f32[512]{0:T(512)S(1)} %fusion.30) | copy-start | bytes 6148
  18.3 95.3 %copy-start.39 = (f32[512,32]{0,1:T(8,128)}, f32[512,32]{0,1:T(8,128)S(1)}, u32[]{:S(2)}) copy-start(f32[512,32]{0,1:T(8,128)S(1)} %get-tuple-element.162) | copy-start | bytes 196612
  18.4 95.3 %copy-start.41 = (f32[512,32]{0,1:T(8,128)}, f32[512,32]{0,1:T(8,128)S(1)}, u32[]{:S(2)}) copy-start(f32[512,32]{0,1:T(8,128)S(1)} %get-tuple-element.163) | copy-start | bytes 196612
  38.2 187.3 %copy-start.52 = (f32[1,1024]{1,0:T(1,128)}, f32[1,1024]{1,0:T(1,128)S(1)}, u32[]{:S(2)}) copy-start(f32[1,1024]{1,0:T(1,128)S(1)} %get-tuple-element.160) | copy-start | bytes 12292
  115.9 7.4 copy-start.23
  115.9 7.4 copy-start.25
  115.9 7.4 copy-start.27
  115.9 7.3 copy-start.29
  123.3 9.6 %copy-start.17 = (bf16[1,512,1024]{1,2,0:T(8,128)(2,1)S(1)}, bf16[1,512,1024]{1,2,0:T(8,128)(2,1)}, u32[]{:S(2)}) copy-start(bf16[1,512,1024]{1,2,0:T(8,128)(2,1)} %copy.69) | copy-start | bytes 3145732
  140.4 3.3 copy-start.60
  143.8 81.7 %copy-start.12 = (f32[512,1024]{1,0:T(8,128)}, f32[512,1024]{1,0:T(8,128)S(1)}, u32[]{:S(2)}) copy-start(f32[512,1024]{1,0:T(8,128)S(1)} %get-tuple-element.167) | copy-start | bytes 6291460
  143.8 81.7 %copy-start.50 = (f32[512]{0:T(512)}, f32[512]{0:T(512)S(1)}, u32[]{:S(2)}) copy-start(f32[512]{0:T(512)S(1)} %broadcast_multiply_fusion.1) | copy-start | bytes 6148
  144.2 81.4 %copy-start.54 = (f32[512]{0:T(512)}, f32[512]{0:T(512)S(1)}, u32[]{:S(2)}) copy-start(f32[512]{0:T(512)S(1)} %fusion.55) | copy-start | bytes 6148
  144.2 88.0 %copy-start.43 = (f32[16,512]{1,0:T(8,128)}, f32[16,512]{1,0:T(8,128)S(1)}, u32[]{:S(2)}) copy-start(f32[16,512]{1,0:T(8,128)S(1)} %log_add_fusion) | copy-start | bytes 98308
  207.3 12.8 %copy-start.59 = (bf16[1024,4096]{1,0:T(8,128)(2,1)S(1)}, bf16[1024,4096]{1,0:T(8,128)(2,1)}, u32[]{:S(2)}) copy-start(bf16[1024,4096]{1,0:T(8,128)(2,1)} %all-gather.9.cloned.1.call-done) | copy-start | bytes 25165828
  220.1 5.4 copy-start.61
  227.6 3.3 copy-start.38
  232.2 24.5 %slice-start = ((s8[16777216]{0:T(1024)(128)(4,1)}), s8[4194304]{0:T(1024)(128)(4,1)S(1)}, s32[]{:S(2)}) async-start(s8[16777216]{0:T(1024)(128)(4,1)} %bitcast.131), calls=%async_computation.13 | async-start | bytes 8388608
  232.2 24.5 %slice-start.1 = ((s8[16777216]{0:T(1024)(128)(4,1)}), s8[4194304]{0:T(1024)(128)(4,1)S(1)}, s32[]{:S(2)}) async-start(s8[16777216]{0:T(1024)(128)(4,1)} %bitcast.131), calls=%async_computation.14 | async-start | bytes 8388608
  242.1 14.6 %slice-start.2 = ((s8[16777216]{0:T(1024)(128)(4,1)}), s8[4194304]{0:T(1024)(128)(4,1)S(1)}, s32[]{:S(2)}) async-start(s8[16777216]{0:T(1024)(128)(4,1)} %bitcast.131), calls=%async_computation.15 | async-start | bytes 8388608
  242.1 14.6 %slice-start.3 = ((s8[16777216]{0:T(1024)(128)(4,1)}), s8[4194304]{0:T(1024)(128)(4,1)S(1)}, s32[]{:S(2)}) async-start(s8[16777216]{0:T(1024)(128)(4,1)} %bitcast.131), calls=%async_computation.16 | async-start | bytes 8388608
  256.7 11.5 %copy-start.28 = (bf16[512,16,32]{0,2,1:T(8,128)(2,1)S(1)}, bf16[512,16,32]{0,2,1:T(8,128)(2,1)}, u32[]{:S(2)}) copy-start(bf16[512,16,32]{0,2,1:T(8,128)(2,1)} %copy-done.27) | copy-start | bytes 1572868
  256.7 11.5 %copy-start.30 = (bf16[512,16,32]{0,2,1:T(8,128)(2,1)S(1)}, bf16[512,16,32]{0,2,1:T(8,128)(2,1)}, u32[]{:S(2)}) copy-start(bf16[512,16,32]{0,2,1:T(8,128)(2,1)} %copy-done.29) | copy-start | bytes 1572868
  265.0 3.2 copy-start
  284.3 7.1 copy-start.49
  295.3 3.3 copy-start.36
  295.3 161.2 %reduce-scatter.5.cloned.1.call-start = ((), (), s32[]{:S(2)}) async-start(), calls=%async_computation.8 | async-start | bytes 18874368 | tf_op jit(solution)/shard_map/reduce_scatter | solution.py:210
  308.8 267.7 %reduce-scatter.9.cloned.1.call-start = ((), (), s32[]{:S(2)}) async-start(), calls=%async_computation.10 | async-start | bytes 18874368 | tf_op jit(solution)/shard_map/reduce_scatter | solution.py:214
  320.9 375.6 %reduce-scatter.11.cloned.1.call-start = ((), (), s32[]{:S(2)}) async-start(), calls=%async_computation.11 | async-start | bytes 18874368 | tf_op jit(solution)/shard_map/reduce_scatter | solution.py:215
  337.2 490.2 %all-reduce.3.cloned.1.call-start = ((), (), s32[]{:S(2)}) async-start(), calls=%async_computation.12 | async-start | bytes 6553600 | tf_op jit(solution)/shard_map/psum | solution.py:218
  707.4 3.0 copy-start.2
  707.4 3.0 copy-start.47
  710.4 3.4 copy-start.14
  725.8 104.2 %copy-start.8 = (f32[4,128,1024]{1,2,0:T(8,128)S(1)}, f32[4,128,1024]{1,2,0:T(8,128)}, u32[]{:S(2)}) copy-start(f32[4,128,1024]{1,2,0:T(8,128)} %copy.85) | copy-start | bytes 6291460
  837.4 3.0 copy-start.10
  845.3 4.4 copy-start.33
  849.7 8.9 %copy-start.6 = (f32[512,1024]{1,0:T(8,128)S(1)}, f32[512,1024]{1,0:T(8,128)}, u32[]{:S(2)}) copy-start(f32[512,1024]{1,0:T(8,128)} %param.36) | copy-start | bytes 6291460
  849.7 8.9 %copy-start.20 = (f32[512,1024]{1,0:T(8,128)S(1)}, f32[512,1024]{1,0:T(8,128)}, u32[]{:S(2)}) copy-start(f32[512,1024]{1,0:T(8,128)} %param.39) | copy-start | bytes 6291460
  849.7 8.9 %copy-start.21 = (f32[512,1024]{1,0:T(8,128)S(1)}, f32[512,1024]{1,0:T(8,128)}, u32[]{:S(2)}) copy-start(f32[512,1024]{1,0:T(8,128)} %param.38) | copy-start | bytes 6291460
  849.7 8.9 %copy-start.22 = (f32[512,1024]{1,0:T(8,128)S(1)}, f32[512,1024]{1,0:T(8,128)}, u32[]{:S(2)}) copy-start(f32[512,1024]{1,0:T(8,128)} %param.37) | copy-start | bytes 6291460
  849.7 8.8 %copy-start.32 = (bf16[512,1024]{1,0:T(8,128)(2,1)S(1)}, bf16[512,1024]{1,0:T(8,128)(2,1)}, u32[]{:S(2)}) copy-start(bf16[512,1024]{1,0:T(8,128)(2,1)} %get-tuple-element.124) | copy-start | bytes 3145732
  (27 other events, 54.6 us)
Sparse Core Ops, SparseCore 0:
  10.5 26.1 all-gather.4
  39.2 54.3 all-gather.6
  96.1 54.3 all-gather.8
  152.8 54.3 all-gather.10
  295.4 41.2 reduce-scatter.6
  340.5 115.9 reduce-scatter.4
  460.5 115.9 reduce-scatter.8
  580.5 115.9 reduce-scatter.10
  701.0 126.3 all-reduce.2
where the time goes:
time: 881 us; the launch traced here: 871 us
  waiting for transfers between devices  579 us (66%)
  matrix products  142 us (16%)
  other arithmetic  81 us (9%)
  local copies, waits for them, and re-layouts  52.8 us (6%)
  between operations  14.8 us (2%)
    reduce_scatter x1, waiting for transfers between devices, local(): lax.psum_scatter(d_down, 'fsdp', scatter_dimension=0, tiled=True)  117 us
    reduce_scatter x1, waiting for transfers between devices, local(): lax.psum_scatter(d_up, 'fsdp', scatter_dimension=0, tiled=True)  117 us
    reduce_scatter x1, waiting for transfers between devices, local(): lax.psum_scatter(d_mixing, 'fsdp', scatter_dimension=1, tiled=True)  117 us
    psum x1, waiting for transfers between devices, local(): lax.psum(mixing_part.astype(jnp.bfloat16), 'rows').astype(jnp.float32)  102 us
    all_gather x1, waiting for transfers between devices, local(): lax.all_gather(mixing_w.astype(jnp.bfloat16), 'fsdp', axis=1, tiled=True)  55.4 us
    all_gather x1, waiting for transfers between devices, local(): lax.all_gather(down_w.astype(jnp.bfloat16), 'fsdp', axis=0, tiled=True)  46.1 us
    unnamed x141, local copies, waits for them, and re-layouts  34.8 us
    add x4, other arithmetic, adam_update(): average_new = 0.8 * average + 0.2 * weight_new  24.4 us
  transfers between devices with their start and end apart: 9, of which 8 were waited for; matrix products, arithmetic and copies ran while one was open for 16% of the time, Pallas kernels for 0%

commit v1 on v0

--- a/solution.py
+++ b/solution.py
@@ -1,12 +1,986 @@
 import jax
 import jax.numpy as jnp
+import numpy as np
 from jax import lax
+from jax.experimental import pallas as pl
+from jax.experimental.pallas import tpu as pltpu
 from jax.sharding import PartitionSpec as P
 
 D = 1024
 HEADS = 16
 HEAD_DIM = 64
 STEP = 7
+F32 = jnp.float32
+BF = jnp.bfloat16
+
+
+MESH = pl.DeviceIdType.MESH
+CHUNKS = 25
+SLOTS = 4
+SIB_SLOTS = 6
+LINE_SLOTS = 6
+LAGS = (1, 3, 5, 7, 9, 11)
+
+
+class Reducer:
+    def __init__(self, refs):
+        (self.away, self.part, self.sib, self.diag, self.near, self.zin, self.zmid, self.tsum, self.out_a, self.out_b,
+         self.sems_sib, self.sems_diag, self.sems_near, self.sems_zin, self.sems_zmid) = refs
+        self.me = lax.axis_index("fsdp")
+        self.core = lax.rem(self.me, 2)
+        self.chip = lax.div(self.me, 2)
+        self.row = lax.axis_index("rows")
+        self.inner = jnp.logical_and(self.row >= 1, self.row <= 2)
+        self.outer = jnp.logical_not(self.inner)
+        self.line_to = jnp.where(self.row == 0, 1, jnp.where(self.row == 1, 0, jnp.where(self.row == 2, 3, 2)))
+        self.mid_to = jnp.where(self.row == 1, 2, 1)
+        xbit = lax.rem(self.chip, 2)
+        ybit = lax.div(self.chip, 2)
+        self.chip_x = ybit * 2 + (1 - xbit)
+        self.chip_y = (1 - ybit) * 2 + xbit
+        self.chip_d = (1 - ybit) * 2 + (1 - xbit)
+        self.to_sib = {"fsdp": self.chip * 2 + (1 - self.core)}
+        self.to_x = {"fsdp": self.chip_x * 2 + self.core}
+        self.to_y = {"fsdp": self.chip_y * 2 + self.core}
+
+    @staticmethod
+    def scratch():
+        s = SLOTS
+        bf = jnp.bfloat16
+        dma = pltpu.SemaphoreType.DMA
+        return [
+            pltpu.VMEM((SIB_SLOTS, 4, 128, 512), bf),
+            pltpu.VMEM((s, 4, 128, 512), bf),
+            pltpu.VMEM((SIB_SLOTS, 4, 128, 512), bf),
+            pltpu.VMEM((s, 128, 512), bf),
+            pltpu.VMEM((s, 2, 128, 512), bf),
+            pltpu.VMEM((LINE_SLOTS, 128, 512), bf),
+            pltpu.VMEM((LINE_SLOTS, 128, 512), bf),
+            pltpu.VMEM((LINE_SLOTS, 128, 512), jnp.float32),
+            pltpu.VMEM((LINE_SLOTS, 128, 512), bf),
+            pltpu.VMEM((LINE_SLOTS, 128, 512), bf),
+            dma((2, SIB_SLOTS)),
+            dma((2, s)),
+            dma((2, s)),
+            dma((2, LINE_SLOTS)),
+            dma((2, LINE_SLOTS)),
+        ]
+
+    def enter(self):
+        barrier = pltpu.get_barrier_semaphore()
+        for to in (self.to_sib, self.to_x, self.to_y, {"rows": self.line_to}):
+            pl.semaphore_signal(barrier, inc=1, device_id=to, device_id_type=MESH)
+
+        @pl.when(self.inner)
+        def _():
+            pl.semaphore_signal(barrier, inc=1, device_id={"rows": self.mid_to}, device_id_type=MESH)
+            pl.semaphore_wait(barrier, 5)
+
+        @pl.when(self.outer)
+        def _():
+            pl.semaphore_wait(barrier, 4)
+
+    def copy(self, src, dst, sems, which, slot, to):
+        return pltpu.make_async_remote_copy(
+            src_ref=src, dst_ref=dst, send_sem=sems.at[which, slot], recv_sem=sems.at[which + sems.shape[0] // 2, slot],
+            device_id=to, device_id_type=MESH)
+
+    def c_sib(self, s):
+        return self.copy(self.away.at[s], self.sib.at[s], self.sems_sib, 0, s, self.to_sib)
+
+    def c_diag(self, s, k):
+        to, half = (self.to_x if k == 0 else self.to_y), pl.ds(64 * k, 64)
+        return self.copy(self.part.at[s, self.chip_d, half], self.diag.at[s, half], self.sems_diag, 0, s, to)
+
+    def c_near(self, s, k):
+        to, chip = (self.to_x, self.chip_x) if k == 0 else (self.to_y, self.chip_y)
+        return self.copy(self.part.at[s, chip], self.near.at[s, k], self.sems_near, 0, s, to)
+
+    def both_diag(self, s):
+        return self.copy(self.part.at[s, self.chip_d], self.diag.at[s], self.sems_diag, 0, s, self.to_x)
+
+    def both_near(self, s):
+        return self.copy(self.part.at[s, pl.ds(0, 2)], self.near.at[s], self.sems_near, 0, s, self.to_x)
+
+    def c_line(self, s):
+        return self.copy(self.out_a.at[s], self.zin.at[s], self.sems_zin, 0, s, {"rows": self.line_to})
+
+    def c_mid(self, s):
+        return self.copy(self.out_b.at[s], self.zmid.at[s], self.sems_zmid, 0, s, {"rows": self.mid_to})
+
+    def stage_b(self, g, keep):
+        s = lax.rem(g, SLOTS)
+        n = lax.rem(g, SIB_SLOTS)
+        self.c_sib(n).wait()
+        keep(g, s, n)
+        self.c_diag(s, 0).start()
+        self.c_diag(s, 1).start()
+
+    def stage_c(self, g):
+        s = lax.rem(g, SLOTS)
+        self.both_diag(s).wait()
+        lo = self.part[s, self.chip_y, :64].astype(jnp.float32) + self.diag[s, :64].astype(jnp.float32)
+        self.part[s, self.chip_y, :64] = lo.astype(jnp.bfloat16)
+        self.c_near(s, 1).start()
+        hi = self.part[s, self.chip_x, 64:].astype(jnp.float32) + self.diag[s, 64:].astype(jnp.float32)
+        self.part[s, self.chip_x, 64:] = hi.astype(jnp.bfloat16)
+        self.c_near(s, 0).start()
+
+    def stage_e(self, g):
+        s = lax.rem(g, SLOTS)
+        self.both_near(s).wait()
+        total = (self.part[s, self.chip].astype(jnp.float32) + self.near[s, 0].astype(jnp.float32)) + self.near[s, 1].astype(jnp.float32)
+        n = lax.rem(g, LINE_SLOTS)
+        self.tsum[n] = total
+
+        @pl.when(self.outer)
+        def _():
+            self.out_a[n] = total.astype(jnp.bfloat16)
+            self.c_line(n).start()
+
+    def stage_f(self, g):
+        s = lax.rem(g, LINE_SLOTS)
+
+        @pl.when(self.inner)
+        def _():
+            self.c_line(s).wait_recv()
+            self.out_b[s] = (self.tsum[s] + self.zin[s].astype(jnp.float32)).astype(jnp.bfloat16)
+            self.c_mid(s).start()
+
+    def stage_h(self, g, put):
+        s = lax.rem(g, LINE_SLOTS)
+
+        @pl.when(self.inner)
+        def _():
+            self.c_mid(s).wait()
+            total = (self.out_b[s].astype(jnp.float32) + self.zmid[s].astype(jnp.float32)).astype(jnp.bfloat16)
+            self.out_a[s] = total
+            self.c_line(s).start()
+            put(g, total)
+
+    def stage_i(self, g, put):
+        s = lax.rem(g, LINE_SLOTS)
+
+        @pl.when(self.outer)
+        def _():
+            self.c_line(s).wait()
+            put(g, self.zin[s])
+
+        @pl.when(self.inner)
+        def _():
+            self.c_line(s).wait_send()
+
+    def tick(self, t, keep, put):
+        b, c, e, f, h, i = LAGS
+
+        def run(lag, stage, *args):
+            g = t - lag
+            pl.when(jnp.logical_and(g >= 0, g < CHUNKS))(lambda: stage(g, *args))
+
+        run(i, self.stage_i, put)
+        run(h, self.stage_h, put)
+        run(f, self.stage_f)
+        run(e, self.stage_e)
+        run(c, self.stage_c)
+        run(b, self.stage_b, keep)
+
+
+def dot(a, b):
+    return lax.dot_general(a, b, (((1,), (0,)), ((), ())), preferred_element_type=F32)
+
+
+def dot_nt(a, b):
+    return lax.dot_general(a, b, (((1,), (1,)), ((), ())), preferred_element_type=F32)
+
+
+START, LINK, SIBLING, HOP, ISSUE, LEAD = 6.0, 50.0, 300.0, 2.0, 0.05, 4.0
+PIECES = [(-1, 0, 1024, True)]
+PIECES += [(k, 512 * h, 512, k == 2 and h == 0) for h in range(2) for k in range(3)]
+PIECES += [(-2, 0, 1024, True), (3, 0, 1024, False)]
+PIECES += [(4 + n, 0, 1024, n in (1, 4, 6, 7)) for n in range(8)]
+COND_TWO, OUT_W, UP_W, DOWN_W = 7, 8, 9, 13
+
+
+SHARED = {4: 3, 5: 0, 6: 0, 7: 0, 9: 8, 10: 8}
+
+
+class Gatherer:
+    def __init__(self, refs):
+        self.cond, self.thirds, self.mats, self.send, self.recv = refs
+        self.me = lax.axis_index("fsdp")
+        core = lax.rem(self.me, 2)
+        chip = lax.div(self.me, 2)
+        xbit, ybit = lax.rem(chip, 2), lax.div(chip, 2)
+        self.x = (ybit * 2 + 1 - xbit) * 2 + core
+        self.y = ((1 - ybit) * 2 + xbit) * 2 + core
+        self.d = ((1 - ybit) * 2 + 1 - xbit) * 2 + core
+        self.sib = chip * 2 + 1 - core
+        row = lax.axis_index("rows")
+        self.half = lax.rem(row, 2)
+        self.to_z = {"rows": row + 1 - 2 * self.half}
+        self.time = START
+        self.free = {"x": 0.0, "y": 0.0, "z": 0.0, "s": 0.0}
+        self.due = {}
+        self.waiting = []
+        self.begun, self.whole = 0, set()
+
+    @staticmethod
+    def scratch():
+        return [
+            pltpu.VMEM((8, 64, 1024), BF),
+            pltpu.VMEM((3, 2, 8, 128, 512), BF),
+            pltpu.VMEM((9, 8, 128, 1024), BF),
+            pltpu.SemaphoreType.DMA((len(PIECES), 11)),
+            pltpu.SemaphoreType.DMA((len(PIECES), 11)),
+        ]
+
+    def enter(self):
+        barrier = pltpu.get_barrier_semaphore()
+        for to in ({"fsdp": self.sib}, {"fsdp": self.x}, {"fsdp": self.y}, self.to_z):
+            pl.semaphore_signal(barrier, inc=1, device_id=to, device_id_type=MESH)
+        pl.semaphore_wait(barrier, 4)
+
+    @staticmethod
+    def direct(c):
+        return PIECES[c][3]
+
+    def shard(self, c, owner, start=0, size=None):
+        mat, col, cols, _ = PIECES[c]
+        if mat < 0:
+            base = 32 * (-1 - mat)
+            return self.cond.at[owner, pl.ds(base + start, 32 if size is None else size)]
+        rows = pl.ds(start, 128 if size is None else size)
+        return self.thirds.at[mat, col // 512, owner, rows] if mat < 3 else self.mats.at[mat - 3, owner, rows]
+
+    def copy(self, c, kind, owner, to, start=0, size=None):
+        ref = self.shard(c, owner, start, size)
+        return pltpu.make_async_remote_copy(
+            src_ref=ref, dst_ref=ref, send_sem=self.send.at[c, kind], recv_sem=self.recv.at[c, SHARED.get(kind, kind)],
+            device_id=to, device_id_type=MESH)
+
+    def landed(self, c, kind, rows):
+        mat, _, cols, _ = PIECES[c]
+        if mat < 0:
+            ref = self.cond.at[pl.ds(0, 4), pl.ds(0, 32)] if rows == 128 else self.cond.at[0, pl.ds(0, rows)]
+        else:
+            base = self.thirds.at[mat, 0] if mat < 3 else self.mats.at[mat - 3]
+            ref = base.at[pl.ds(0, rows // 128)] if rows >= 128 else base.at[0, pl.ds(0, rows)]
+            if rows == 192:
+                ref = base.at[pl.ds(0, 3), pl.ds(0, 64)]
+        pltpu.make_async_remote_copy(
+            src_ref=ref, dst_ref=ref, send_sem=self.send.at[c, kind], recv_sem=self.recv.at[c, kind],
+            device_id={"fsdp": self.sib}, device_id_type=MESH).wait_recv()
+
+    def span(self, c, k=None):
+        rows = 32 if PIECES[c][0] < 0 else 128
+        if self.direct(c):
+            return (0, None) if k is None else (k * (rows // 2), rows // 2)
+        return (self.half * 64, 64) if k is None else (self.half * 64 + 32 * k, 32)
+
+    def post(self, link, mark, copy):
+        copy.start()
+        rows, cols = copy.src_ref.shape[-2:]
+        self.time += ISSUE
+        self.free[link] = max(self.free[link], self.time) + rows * cols * 2e-3 / (SIBLING if link == "s" else LINK)
+        self.due[mark] = self.free[link] + HOP
+
+    def take(self, mark, copy):
+        copy.wait_recv()
+        self.time = max(self.time, self.due[mark]) + ISSUE
+
+    def take_all(self, c, kinds, rows):
+        self.landed(c, kinds[0], rows)
+        self.time = max([self.time] + [self.due[c, kind] for kind in kinds]) + ISSUE
+
+    def onward(self, c, kind, owner):
+        if self.direct(c):
+            self.post("s", (c, 5 + kind), self.copy(c, 5 + kind, owner, {"fsdp": self.sib}))
+        else:
+            self.post("z", (c, 8 + kind), self.copy(c, 8 + kind, owner, self.to_z, *self.span(c)))
+
+    def s1(self, c):
+        self.post("x", (c, 1), self.copy(c, 1, self.me, {"fsdp": self.x}, *self.span(c)))
+        self.post("y", (c, 2), self.copy(c, 2, self.me, {"fsdp": self.y}, *self.span(c)))
+        self.post("s", (c, 0), self.copy(c, 0, self.me, {"fsdp": self.sib}))
+        self.begun = c + 1
+        self.waiting.append((2, c))
+
+    def s2(self, c):
+        self.take((c, 1), self.copy(c, 1, self.x, {"fsdp": self.x}, *self.span(c)))
+        self.post("y", (c, 3), self.copy(c, 3, self.x, {"fsdp": self.y}, *self.span(c, 0)))
+        self.onward(c, 0, self.x)
+        self.take((c, 2), self.copy(c, 2, self.y, {"fsdp": self.y}, *self.span(c)))
+        self.post("x", (c, 4), self.copy(c, 4, self.y, {"fsdp": self.x}, *self.span(c, 1)))
+        self.onward(c, 1, self.y)
+        self.waiting.append((3, c))
+
+    def s3(self, c):
+        self.take_all(c, (3, 4), self.moved(c))
+        self.onward(c, 2, self.d)
+        self.waiting.append((5 if self.direct(c) else 4, c))
+
+    def s4(self, c):
+        self.take_all(c, (8, 9, 10), 192)
+        for kind, owner in enumerate((self.x, self.y, self.d)):
+            self.post("s", (c, 5 + kind), self.copy(c, 5 + kind, owner, {"fsdp": self.sib}))
+        self.waiting.append((5, c))
+
+    def moved(self, c):
+        rows = 32 if PIECES[c][0] < 0 else 128
+        return rows if self.direct(c) else rows // 2
+
+    def s5(self, c):
+        self.take_all(c, (0, 5, 6, 7), 128 if PIECES[c][0] < 0 else 512)
+        self.whole.add(c)
+
+    def ready(self, event):
+        stage, c = event
+        marks = {2: (1, 2), 3: (3, 4), 4: (8, 9, 10), 5: (0, 5, 6, 7)}[stage]
+        return max(self.due[c, kind] for kind in marks)
+
+    def feed(self):
+        while self.begun < len(PIECES) and min(self.free["x"], self.free["y"]) - self.time < LEAD:
+            self.s1(self.begun)
+
+    def step(self, event):
+        self.waiting.remove(event)
+        stage, c = event
+        (self.s2, self.s3, self.s4, self.s5)[stage - 2](c)
+
+    def spend(self, time):
+        self.time += time
+        while True:
+            self.feed()
+            landed = [event for event in self.waiting if self.ready(event) <= self.time]
+            if not landed:
+                break
+            self.step(min(landed, key=lambda event: (self.ready(event), event)))
+
+    def need(self, c):
+        while c not in self.whole:
+            self.feed()
+            self.step(min(self.waiting, key=lambda event: (self.ready(event), event)))
+
+    def finish(self):
+        for c in range(len(PIECES)):
+            self.copy(c, 0, self.me, {"fsdp": self.sib}).wait_send()
+            for kind in (1, 2):
+                self.copy(c, kind, self.me, {"fsdp": self.x}, *self.span(c)).wait_send()
+            for k in range(2):
+                self.copy(c, 3 + k, self.x, {"fsdp": self.x}, *self.span(c, k)).wait_send()
+            for kind in range(3):
+                self.copy(c, 5 + kind, self.x, {"fsdp": self.sib}).wait_send()
+                if not self.direct(c):
+                    self.copy(c, 8 + kind, self.x, self.to_z, *self.span(c)).wait_send()
+
+
+def forward_kernel(
+    seg_in, freq_in, te_in, x_in, cot_hbm, mixing_hbm, cond_hbm, up_hbm, down_hbm,
+    lse_out, scales_out, turn_out, feat_out, thirds_hbm, w_hbm, lt_hbm, dpre_hbm, qkv_hbm, mid_hbm, back_hbm, out_hbm,
+    four, wide, condf, nrm, qkv, att, mid, te_at, act, cot, ltb, gbuf, eye, in_sem, w_sem, lt_sem, g_sem, o_sem, *shared,
+):
+    gat = Gatherer(shared)
+    me = gat.me
+    thirds, mats = gat.thirds, gat.mats
+
+    def load(src, dst, n):
+        return pltpu.make_async_copy(src, dst, in_sem.at[n])
+
+    loads = [load(cond_hbm, condf, 0)]
+    loads += [load(mixing_hbm.at[k], four.at[k], 1 + k) for k in range(4)]
+    loads += [load(up_hbm, wide, 5), load(cot_hbm, cot, 6)]
+    for copy in loads:
+        copy.start()
+    gat.enter()
+    obuf = att
+    loads[0].wait()
+    for k in range(2):
+        gat.cond[me, 32 * k:32 * k + 32] = condf[k].astype(BF)
+    gat.s1(0)
+    for k in range(4):
+        loads[1 + k].wait()
+        if k < 3:
+            for h in range(2):
+                thirds[k, h, me] = four[k, :, 512 * h:512 * h + 512].astype(BF)
+            if k < 2:
+                gat.s1(1 + k)
+        else:
+            mats[0, me] = four[k].astype(BF)
+    later = [load(down_hbm.at[pl.ds(128 * i, 128)], four.at[i], 7 + i) for i in range(4)]
+    for copy in later:
+        copy.start()
+    ids = seg_in[...].astype(F32)
+    column = jnp.broadcast_to(ids, (128, 512)).T[:, :1]
+    before = jnp.sum(jnp.where(ids < column, 1.0, 0.0), axis=1, keepdims=True)
+    offset = lax.broadcasted_iota(jnp.int32, (512, 1), 0).astype(F32) - before
+    angle = offset * freq_in[...]
+    lanes = lax.broadcasted_iota(jnp.int32, (1, 128), 1)
+    lane_in = lax.rem(lanes, 64)
+    low_half = lane_in < 32
+    turn_out[0] = jnp.cos(angle)
+    turn_out[1] = jnp.where(low_half, -1.0, 1.0) * jnp.sin(angle)
+    spot = lane_in.astype(F32)
+    square = (lax.broadcasted_iota(jnp.int32, (256, 256), n) for n in range(2))
+    eye[...] = jnp.where(next(square) == next(square), 1.0, 0.0).astype(BF)
+    feat_out[0] = jnp.where(jnp.logical_and(lane_in < 4, spot != column), 1.0, 0.0).astype(BF)
+    feat_out[1] = jnp.where(spot == column, -1e30, 0.0).astype(BF)
+    te_column = jnp.broadcast_to(te_in[...].astype(F32), (128, 256)).T[:, :1]
+    for f in range(8):
+        te_at[f] = te_column[32 * f:32 * f + 32]
+    loads[5].wait()
+    for i in range(4):
+        for f in range(8):
+            mats[1 + i, me, :, 128 * f:128 * f + 128] = wide[:, 512 * f + 128 * i:512 * f + 128 * i + 128].astype(BF)
+    for i in range(4):
+        later[i].wait()
+        mats[5 + i, me] = four[i].astype(BF)
+
+    def save_w(m):
+        if m < 3:
+            return pltpu.make_async_copy(thirds.at[m], thirds_hbm.at[m], w_sem.at[m])
+        return pltpu.make_async_copy(mats.at[0], w_hbm, w_sem.at[m])
+
+    def save_lt(n, slot):
+        return pltpu.make_async_copy(ltb.at[slot], lt_hbm.at[n], lt_sem.at[slot])
+
+    def turn(block, b, slot):
+        rows = slice(128 * b, 128 * b + 128) if isinstance(b, int) else pl.ds(pl.multiple_of(b * 128, 128), 128)
+        turned = dot_nt(eye[...], block).astype(BF)
+        for a in range(2):
+            ltb[slot, a, rows] = turned[128 * a:128 * a + 128]
+
+    def scale_of(k):
+        total = jnp.zeros((32, 1024), F32)
+        for f in range(8):
+            total = total + te_at[f] * gat.cond[f, 32 * k:32 * k + 32].astype(F32)
+        scales_out[k:k + 1] = 1.0 + jnp.sum(total, axis=0, keepdims=True)
+
+    def norm_rows(source, scale):
+        def block(b, carry):
+            rows = pl.ds(pl.multiple_of(b * 64, 64), 64)
+            values = source[rows].astype(F32)
+            center = values - jnp.mean(values, axis=-1, keepdims=True)
+            spread = jnp.mean(center * center, axis=-1, keepdims=True)
+            nrm[rows] = (center * lax.rsqrt(spread + 1e-05) * scale).astype(BF)
+            return carry
+
+        lax.fori_loop(0, 8, block, 0, unroll=2)
+
+    gat.need(0)
+    scale_of(0)
+    norm_rows(x_in, scales_out[0:1])
+    gat.spend(1.2)
+
+    def save_qkv(k):
+        return pltpu.make_async_copy(qkv.at[k], qkv_hbm.at[k], o_sem.at[k])
+
+    def project(k, half):
+        at = slice(512 * half, 512 * half + 512)
+        result = dot(nrm[...], thirds[k, half].reshape(1024, 512))
+        if k == 0:
+            for b in range(2):
+                turn(nrm[:, 512 * half + 256 * b:512 * half + 256 * b + 256], 2 * half + b, 0)
+        if k < 2:
+            sides = []
+            for n in range(4):
+                part = result[:, 128 * n:128 * n + 128]
+                other = jnp.where(low_half, pltpu.roll(part, 96, 1), pltpu.roll(part, 32, 1))
+                sides.append(part * turn_out[0] + other * turn_out[1])
+            result = jnp.concatenate(sides, axis=1)
+        result = result.astype(BF)
+        qkv[k, :, at] = result * jnp.asarray(0.125, BF) if k == 0 else result
+
+    def attend(pair, carry):
+        at = pl.ds(pl.multiple_of(pair * 128, 128), 128)
+        q_pair, k_pair = qkv[0, :, at], qkv[1, :, at]
+        v_turned = qkv[2, :, at].T
+        heads = [lax.div(lanes, 64) == j for j in range(2)]
+        raws = [dot_nt(jnp.where(mine, k_pair, feat_out[1]), jnp.where(mine, q_pair, feat_out[0])) for mine in heads]
+        peaks = [jnp.max(raw, axis=0, keepdims=True) for raw in raws]
+        grown = [jnp.exp(raw - peak) for raw, peak in zip(raws, peaks)]
+        totals = [jnp.sum(value, axis=0, keepdims=True) for value in grown]
+        sides = [dot(v_turned[64 * j:64 * j + 64], grown[j].astype(BF)) * (1.0 / totals[j]) for j in range(2)]
+        sums = [peak + jnp.log(total) for peak, total in zip(peaks, totals)]
+        lse_out[pair] = jnp.concatenate(sums, axis=0)
+        block = jnp.concatenate(sides, axis=0).astype(BF)
+        ltb[1, lax.rem(pair, 2), pl.ds(pl.multiple_of(lax.div(pair, 2) * 128, 128), 128)] = block
+        att[:, at] = block.T
+        return carry
+
+    for half in range(2):
+        for k in range(3):
+            gat.need(1 + 3 * half + k)
+            project(k, half)
+            gat.spend(0.9)
+        if half == 1:
+            for k in range(3):
+                save_w(k).start()
+                save_qkv(k).start()
+            save_lt(6, 0).start()
+        for part in range(2):
+            begin = 4 * half + 2 * part
+            lax.fori_loop(begin, begin + 2, attend, 0)
+            gat.spend(3.6)
+    save_lt(5, 1).start()
+    gat.need(COND_TWO)
+    scale_of(1)
+    gat.need(OUT_W)
+    save_w(3).start()
+
+    def join(b, carry):
+        at = pl.ds(pl.multiple_of(b * 512, 512), 512)
+        mid[:, at] = x_in[:, at].astype(F32) + dot(att[...], mats[0, :, :, at].reshape(1024, 512))
+        return carry
+
+    lax.fori_loop(0, 2, join, 0)
+    gat.spend(1.8)
+    save_mid = pltpu.make_async_copy(mid, mid_hbm, o_sem.at[3])
+    save_mid.start()
+    norm_rows(mid, scales_out[1:2])
+    gat.spend(2.4)
+    befores = {0: 6, 1: 5, 2: 4}
+
+    def save_dpre(i):
+        return pltpu.make_async_copy(gbuf.at[i], dpre_hbm.at[i], g_sem.at[i])
+
+    for i in range(4):
+        gat.need(UP_W + i)
+        save_lt(befores[i % 3], i % 3).wait()
+
+        def expand(b, carry):
+            at = pl.ds(pl.multiple_of(b * 512, 512), 512)
+            u = dot(nrm[...], mats[1 + i, :, :, at].reshape(1024, 512))
+            root = 0.7978845608028654
+            square = u * u
+            bend = jnp.tanh(root * u * (1.0 + 0.044715 * square))
+            side = 0.5 * (1.0 + bend)
+            result = (u * side).astype(BF)
+            act[i, :, at] = result
+            for n in range(2):
+                turn(result[:, 256 * n:256 * n + 256], 2 * b + n, i % 3)
+                if i == 0:
+                    turn(nrm[:, pl.ds(pl.multiple_of(b * 512 + n * 256, 256), 256)], 2 * b + n, 2)
+            slope = side + 0.5 * u * (1.0 - bend * bend) * (root * (1.0 + 3.0 * 0.044715 * square))
+            gbuf[i, :, at] = slope.astype(BF)
+            return carry
+
+        lax.fori_loop(0, 2, expand, 0)
+        save_lt(i, i % 3).start()
+        befores[i % 3] = i
+        if i == 0:
+            save_lt(4, 2).start()
+        gat.spend(3.0)
+    for i in range(4):
+        gat.need(DOWN_W + i)
+        if i == 0:
+            loads[6].wait()
+
+        def slopes(b, carry):
+            at = pl.ds(pl.multiple_of(b * 512, 512), 512)
+            d_act = dot_nt(cot[...], mats[5 + i, pl.ds(4 * b, 4)].reshape(512, 1024))
+            gbuf[i, :, at] = (d_act * gbuf[i, :, at].astype(F32)).astype(BF)
+            return carry
+
+        lax.fori_loop(0, 2, slopes, 0)
+        save_dpre(i).start()
+        gat.spend(1.2)
+
+    def shrink(b, carry):
+        at = pl.ds(pl.multiple_of(b * 512, 512), 512)
+        total = mid[:, at]
+        for i in range(4):
+            total = total + dot(act[i], mats[5 + i, :, :, at].reshape(1024, 512))
+        obuf[:, at] = total.astype(BF)
+        back = dot_nt(gbuf[0], mats[1, pl.ds(4 * b, 4)].reshape(512, 1024))
+        for i in range(1, 4):
+            back = back + dot_nt(gbuf[i], mats[1 + i, pl.ds(4 * b, 4)].reshape(512, 1024))
+        four[:, :, at] = back.reshape(4, 128, 512)
+        return carry
+
+    lax.fori_loop(0, 2, shrink, 0)
+    save_out = pltpu.make_async_copy(obuf, out_hbm, o_sem.at[4])
+    save_out.start()
+    save_back = pltpu.make_async_copy(four, back_hbm, o_sem.at[5])
+    save_back.start()
+    gat.finish()
+    for m in range(4):
+        save_w(m).wait()
+    for k in range(3):
+        save_qkv(k).wait()
+        save_lt(befores[k], k).wait()
+    save_mid.wait()
+    for i in range(4):
+        save_dpre(i).wait()
+    save_out.wait()
+    save_back.wait()
+
+
+def forward(seg, te, x, cot, mixing_w, cond_w, up_w, down_w):
+    vmem = pl.BlockSpec(memory_space=pltpu.VMEM)
+    anyw = pl.BlockSpec(memory_space=pl.ANY)
+    shape = jax.ShapeDtypeStruct
+    freq = 10000.0 ** (-(np.arange(128) % 32) * 2.0 / HEAD_DIM)
+    return pl.pallas_call(
+        forward_kernel,
+        out_shape=(
+            shape((8, 2, 512), F32), shape((2, 1024), F32), shape((2, 512, 128), F32), shape((2, 512, 128), BF),
+            shape((3, 2, 8, 128, 512), BF), shape((8, 128, 1024), BF), shape((7, 2, 512, 512), BF), shape((4, 512, 1024), BF),
+            shape((3, 512, 1024), BF), shape((512, 1024), F32), shape((4, 128, 1024), F32), shape((512, 1024), BF)),
+        in_specs=[vmem] * 4 + [anyw] * 5,
+        out_specs=(vmem,) * 4 + (anyw,) * 8,
+        scratch_shapes=[
+            pltpu.VMEM((4, 128, 1024), F32),
+            pltpu.VMEM((128, 4096), F32),
+            pltpu.VMEM((2, 32, 1024), F32),
+            pltpu.VMEM((512, 1024), BF),
+            pltpu.VMEM((3, 512, 1024), BF),
+            pltpu.VMEM((512, 1024), BF),
+            pltpu.VMEM((512, 1024), F32),
+            pltpu.VMEM((8, 32, 1), F32),
+            pltpu.VMEM((4, 512, 1024), BF),
+            pltpu.VMEM((512, 1024), BF),
+            pltpu.VMEM((3, 2, 512, 512), BF),
+            pltpu.VMEM((4, 512, 1024), BF),
+            pltpu.VMEM((256, 256), BF),
+            pltpu.SemaphoreType.DMA((11,)),
+            pltpu.SemaphoreType.DMA((4,)),
+            pltpu.SemaphoreType.DMA((3,)),
+            pltpu.SemaphoreType.DMA((4,)),
+            pltpu.SemaphoreType.DMA((6,)),
+        ] + Gatherer.scratch(),
+        compiler_params=pltpu.CompilerParams(collective_id=2, has_side_effects=True, vmem_limit_bytes=63 * 2**20),
+    )(seg, jnp.asarray(freq[None], F32), te, x, cot, mixing_w, cond_w, up_w, down_w)
+
+
+def norm_back(values, grads, scale):
+    center = values - jnp.mean(values, axis=-1, keepdims=True)
+    recip = lax.rsqrt(jnp.mean(center * center, axis=-1, keepdims=True) + 1e-05)
+    unit = center * recip
+    g = grads * scale
+    back = recip * (g - jnp.mean(g, axis=-1, keepdims=True) - unit * jnp.mean(g * unit, axis=-1, keepdims=True))
+    return back, grads * unit
+
+
+def backward_kernel(
+    turn_in, lse_in, scales_in, te_in, feat_in, thirds_hbm, w_hbm, lt_hbm, cot_hbm, dpre_hbm, qkv_hbm, mid_hbm, back_hbm, x_hbm,
+    sums, in_grad,
+    lt, rh, thirds, wout, qkv, mid, acc, dmid, datt, xin, dscale, obuf, te_at, load_sem, out_sem, *shared,
+):
+    red = Reducer(shared)
+    core = red.core
+
+    def load(src, dst, n):
+        return pltpu.make_async_copy(src, dst, load_sem.at[n])
+
+    load_lt = [load(lt_hbm.at[n], lt.at[n], n) for n in range(7)]
+    load_cot = load(cot_hbm, rh.at[0], 7)
+    load_mid = load(mid_hbm, mid, 8)
+    load_back = load(back_hbm, acc, 9)
+    load_w3 = load(w_hbm, wout, 10)
+    load_qkv = load(qkv_hbm, qkv, 11)
+    load_dpre = load(dpre_hbm, rh.at[pl.ds(1, 4)], 12)
+    load_w = load(thirds_hbm, thirds, 13)
+    load_x = load(x_hbm, xin, 14)
+    for copy in (load_cot, load_lt[0], load_mid, load_back, load_w3):
+        copy.start()
+    later = (load_lt[1], load_qkv, load_lt[2], load_lt[3], load_lt[4], load_dpre, load_lt[5], load_w, load_lt[6], load_x)
+    arrivals = {1: (load_lt[1], load_qkv), 2: (load_lt[2],), 3: (load_lt[3],), 4: (load_lt[4], load_dpre), 8: (load_lt[5],),
+                9: (load_lt[6], load_w, load_x)}
+    red.enter()
+
+    def operands(g):
+        left = jnp.where(g < 8, lax.div(g, 2), jnp.where(g < 16, 4, jnp.where(g < 18, 5, 6)))
+        right = jnp.where(g < 8, 0, jnp.where(g < 16, 1 + lax.div(g - 8, 2), jnp.where(g < 18, 5, 6 + lax.div(g - 18, 2))))
+        return left, rh[right, :, pl.ds(pl.multiple_of(lax.rem(g, 2) * 512, 512), 512)]
+
+    def give(g):
+        left, right = operands(g)
+        n = lax.rem(g, SIB_SLOTS)
+        red.away[n] = dot(lt[left, 1 - core], right).astype(BF).reshape(4, 128, 512)
+        red.c_sib(n).start()
+
+    def cond_part(parity):
+        rows = []
+        for chip in range(4):
+            column = te_at[2 * chip + parity]
+            rows.append(jnp.concatenate([column * dscale[k:k + 1, 512 * h:512 * h + 512] for k in range(2) for h in range(2)], axis=0)[None])
+        return jnp.concatenate(rows, axis=0)
+
+    def keep(g, s, n):
+        @pl.when(g < CHUNKS - 1)
+        def _():
+            left, right = operands(g)
+            own = dot(lt[left, core], right).reshape(4, 128, 512)
+            red.part[s] = (own + red.sib[n].astype(F32)).astype(BF)
+
+        @pl.when(g == CHUNKS - 1)
+        def _():
+            red.part[s] = (cond_part(core) + red.sib[n].astype(F32)).astype(BF)
+
+    def put(g, value):
+        sums[g] = value
+
+    te_column = jnp.broadcast_to(te_in[...].astype(F32), (128, 256)).T[:, :1]
+    for f in range(8):
+        te_at[f] = te_column[32 * f:32 * f + 32]
+    lanes = lax.broadcasted_iota(jnp.int32, (1, 128), 1)
+    low_half = lax.rem(lanes, 64) < 32
+
+    def unrotate(block):
+        other = jnp.where(low_half, pltpu.roll(block, 96, 1), pltpu.roll(block, 32, 1))
+        return block * turn_in[0] - other * turn_in[1]
+
+    def middle_back():
+        for copy in later:
+            copy.start()
+        load_mid.wait()
+        load_back.wait()
+
+        def norm_two(b, total):
+            rows = pl.ds(pl.multiple_of(b * 64, 64), 64)
+            back, terms = norm_back(mid[rows], acc[rows], scales_in[1:2])
+            back = back + rh[0, rows].astype(F32)
+            dmid[rows] = back
+            rh[5, rows] = back.astype(BF)
+            return total + jnp.sum(terms.reshape(8, 8, 1024), axis=0)
+
+        total = lax.fori_loop(0, 8, norm_two, jnp.zeros((8, 1024), F32), unroll=2)
+        dscale[1:2] = jnp.sum(total, axis=0, keepdims=True)
+        load_w3.wait()
+        for n in range(2):
+            cols = slice(512 * n, 512 * n + 512)
+            datt[:, cols] = dot_nt(rh[5], wout[cols, :]).astype(BF)
+
+    def attend_back(pair):
+        at = pl.ds(pl.multiple_of(pair * 128, 128), 128)
+        q_pair, k_pair, v_pair, d_pair = qkv[0, :, at], qkv[1, :, at], qkv[2, :, at], datt[:, at]
+        k_turned = (k_pair * jnp.asarray(0.125, BF)).T
+        heads = [lax.div(lanes, 64) == j for j in range(2)]
+        raws = [dot_nt(jnp.where(mine, k_pair, feat_in[1]), jnp.where(mine, q_pair, feat_in[0])) for mine in heads]
+        d_probs = [dot_nt(v_pair, jnp.where(mine, d_pair, jnp.zeros_like(d_pair))) for mine in heads]
+        made = []
+        for j in range(2):
+            probs = jnp.exp(raws[j] - lse_in[pair, j:j + 1])
+            delta = jnp.sum(probs * d_probs[j], axis=0, keepdims=True)
+            d_raw = (probs * (d_probs[j] - delta)).astype(BF)
+            made.append((dot(k_turned[64 * j:64 * j + 64], d_raw), dot(d_raw, q_pair), dot(probs.astype(BF), d_pair)))
+        rh[6, :, at] = unrotate(jnp.concatenate([made[0][0], made[1][0]], axis=0).T).astype(BF)
+        rh[7, :, at] = unrotate(jnp.where(heads[0], made[0][1], made[1][1])).astype(BF)
+        rh[8, :, at] = jnp.where(heads[0], made[0][2], made[1][2]).astype(BF)
+
+    def first_back(k):
+        for h in range(2):
+            cols = slice(512 * h, 512 * h + 512)
+            part = dot_nt(rh[6 + k, :, :512], thirds[k, 0, cols]) + dot_nt(rh[6 + k, :, 512:], thirds[k, 1, cols])
+
+            @pl.when(k == 0)
+            def _():
+                acc[:, cols] = part
+
+            @pl.when(k > 0)
+            def _():
+                acc[:, cols] += part
+
+    def input_back():
+        def norm_one(b, total):
+            rows = pl.ds(pl.multiple_of(b * 64, 64), 64)
+            back, terms = norm_back(xin[rows].astype(F32), acc[rows], scales_in[0:1])
+            obuf[rows] = (dmid[rows] + back).astype(BF)
+            return total + jnp.sum(terms.reshape(8, 8, 1024), axis=0)
+
+        total = lax.fori_loop(0, 8, norm_one, jnp.zeros((8, 1024), F32), unroll=2)
+        dscale[0:1] = jnp.sum(total, axis=0, keepdims=True)
+        store_out.start()
+        n = (CHUNKS - 1) % SIB_SLOTS
+        red.away[n] = cond_part(1 - core).astype(BF)
+        red.c_sib(n).start()
+
+    store_out = pltpu.make_async_copy(obuf, in_grad, out_sem)
+    load_cot.wait()
+    load_lt[0].wait()
+
+    def turn(m, carry):
+        for when, copies in arrivals.items():
+            @pl.when(m == when)
+            def _(copies=copies):
+                for copy in copies:
+                    copy.wait()
+
+        @pl.when(m < 12)
+        def _():
+            give(2 * m)
+            give(2 * m + 1)
+
+        pl.when(m == 0)(middle_back)
+        pl.when(jnp.logical_and(m >= 1, m < 9))(lambda: attend_back(m - 1))
+
+        pl.when(jnp.logical_and(m >= 9, m < 12))(lambda: first_back(m - 9))
+        pl.when(m == 12)(input_back)
+        def ticks(t, carry):
+            red.tick(t, keep, put)
+            return carry
+
+        lax.fori_loop(2 * m, 2 * m + 2, ticks, 0)
+
+        return carry
+
+    lax.fori_loop(0, (CHUNKS + LAGS[-1] + 1) // 2, turn, 0)
+    store_out.wait()
+
+
+def backward(turn, lse, scales, te, feat, thirds, w, lt, cot, dpre, qkv, mid, back, x):
+    vmem = pl.BlockSpec(memory_space=pltpu.VMEM)
+    anyw = pl.BlockSpec(memory_space=pl.ANY)
+    shape = jax.ShapeDtypeStruct
+    return pl.pallas_call(
+        backward_kernel,
+        out_shape=(
+            shape((CHUNKS, 128, 512), BF), shape((512, 1024), BF)),
+        in_specs=[vmem] * 5 + [anyw] * 9,
+        out_specs=(vmem, anyw),
+        scratch_shapes=[
+            pltpu.VMEM((7, 2, 512, 512), BF),
+            pltpu.VMEM((9, 512, 1024), BF),
+            pltpu.VMEM((3, 2, 1024, 512), BF),
+            pltpu.VMEM((1024, 1024), BF),
+            pltpu.VMEM((3, 512, 1024), BF),
+            pltpu.VMEM((512, 1024), F32),
+            pltpu.VMEM((512, 1024), F32),
+            pltpu.VMEM((512, 1024), F32),
+            pltpu.VMEM((512, 1024), BF),
+            pltpu.VMEM((512, 1024), BF),
+            pltpu.VMEM((2, 1024), F32),
+            pltpu.VMEM((512, 1024), BF),
+            pltpu.VMEM((8, 32, 1), F32),
+            pltpu.SemaphoreType.DMA((16,)),
+            pltpu.SemaphoreType.DMA,
+        ] + Reducer.scratch(),
+        compiler_params=pltpu.CompilerParams(collective_id=1, has_side_effects=True, vmem_limit_bytes=63 * 2**20),
+    )(turn, lse, scales, te, feat, thirds.reshape(3, 2, 1024, 512), w.reshape(1024, 1024), lt, cot, dpre, qkv, mid, back.reshape(512, 1024), x)
+
+
+def update_kernel(*refs):
+    sums, states, rows, outs, rows_out = refs[0], refs[1:17], refs[17:19], refs[19:39], refs[39:41]
+    fresh, held, made, passed, in_sem, out_sem, pass_sem = refs[41:]
+    mix, cond, up, down = range(4)
+    units = [(kind, i) for kind in (down, up, mix) for i in range(4)] + [(cond, 0)]
+    keep_one = 1.0 / (1.0 - 0.5**STEP)
+
+    def piece(ref, kind, i):
+        if kind == up:
+            return ref.at[:, pl.ds(1024 * i, 1024)]
+        if kind == cond:
+            return ref
+        return ref.at[i] if len(ref.shape) == 3 else ref.at[pl.ds(128 * i, 128)]
+
+    def summed(kind, i, buffer):
+        if kind == cond:
+            return [(sums.at[24, pl.ds(64 * k + 32 * h, 32)], buffer.at[pl.ds(32 * k, 32), pl.ds(512 * h, 512)])
+                    for k in range(2) for h in range(2)]
+        if kind == up:
+            half, first = i // 2, 2 * (i % 2)
+            return [(sums.at[8 + 2 * n + half, :, pl.ds(128 * (first + a), 128)], buffer.at[:, pl.ds(512 * a + 128 * n, 128)])
+                    for n in range(4) for a in range(2)]
+        chunk = 2 * i if kind == down else 16 + 2 * ((i + 1) % 4)
+        return [(sums.at[chunk + h], buffer.at[:, pl.ds(512 * h, 512)]) for h in range(2)]
+
+    def loads(u):
+        kind, i = units[u]
+        s = u % RING
+        copies = [(a, b, in_sem.at[s, 8 + n]) for n, (a, b) in enumerate(summed(kind, i, fresh.at[s]))]
+        for n, ref in enumerate(states[4 * kind:4 * kind + 4]):
+            if kind == cond:
+                for k in range(2):
+                    copies.append((ref.at[k], held.at[s, n, pl.ds(32 * k, 32)], in_sem.at[s, 4 * k + n]))
+            else:
+                copies.append((piece(ref, kind, i), held.at[s, n], in_sem.at[s, n]))
+        return [pltpu.make_async_copy(*c) for c in copies]
+
+    def saves(u):
+        kind, i = units[u]
+        s = u % RING
+        copies = []
+        for n in range(5):
+            ref, buffer = outs[5 * kind + n], made.at[s, n]
+            if kind == cond:
+                for k in range(2):
+                    copies.append((buffer.at[pl.ds(32 * k, 32)], ref.at[k], out_sem.at[s, 5 * k + n]))
+            else:
+                copies.append((buffer, piece(ref, kind, i), out_sem.at[s, n]))
+        return [pltpu.make_async_copy(*c) for c in copies]
+
+    enter = [pltpu.make_async_copy(rows[n], passed.at[n], pass_sem.at[n]) for n in range(2)]
+    leave = [pltpu.make_async_copy(passed.at[n], rows_out[n].at[0], pass_sem.at[n]) for n in range(2)]
+    for u in range(RING - 1):
+        for copy in loads(u):
+            copy.start()
+    for copy in enter:
+        copy.start()
+    for u in range(len(units)):
+        s = u % RING
+        if u == 2:
+            for n in range(2):
+                enter[n].wait()
+                leave[n].start()
+        if u + RING - 1 < len(units):
+            for copy in loads(u + RING - 1):
+                copy.start()
+        if u >= RING:
+            for copy in saves(u - RING):
+                copy.wait()
+        for copy in loads(u):
+            copy.wait()
+
+        def rows_step(b, carry):
+            rows = pl.ds(pl.multiple_of(b * 16, 16), 16)
+            g = fresh[s, rows].astype(F32)
+            w = held[s, 0, rows]
+            m = 0.5 * held[s, 1, rows] + 0.5 * g
+            v = 0.5 * held[s, 2, rows] + 0.5 * g * g
+            w_new = w - 0.01 * (m * keep_one / (jnp.sqrt(v * keep_one) + 1e-08) + 0.1 * w)
+            made[s, 0, rows] = g
+            made[s, 1, rows] = m
+            made[s, 2, rows] = v
+            made[s, 3, rows] = w_new
+            made[s, 4, rows] = 0.8 * held[s, 3, rows] + 0.2 * w_new
+            return carry
+
+        lax.fori_loop(0, 4 if units[u][0] == cond else 8, rows_step, 0)
+        for copy in saves(u):
+            copy.start()
+    for u in range(len(units) - RING, len(units)):
+        for copy in saves(u):
+            copy.wait()
+    for copy in leave:
+        copy.wait()
+
+
+RING = 4
+
+
+def update(sums, states, rows):
+    anyw = pl.BlockSpec(memory_space=pl.ANY)
+    outs = []
+    for n in range(4):
+        outs += [jax.ShapeDtypeStruct(states[4 * n].shape, F32)] * 5
+    outs += [jax.ShapeDtypeStruct((1, 512, 1024), BF)] * 2
+    *made, output, input_grad = pl.pallas_call(
+        update_kernel,
+        out_shape=tuple(outs),
+        in_specs=[anyw] * 19,
+        out_specs=(anyw,) * 22,
+        scratch_shapes=[
+            pltpu.VMEM((RING, 128, 1024), BF),
+            pltpu.VMEM((RING, 4, 128, 1024), F32),
+            pltpu.VMEM((RING, 5, 128, 1024), F32),
+            pltpu.VMEM((2, 512, 1024), BF),
+            pltpu.SemaphoreType.DMA((RING, 16)),
+            pltpu.SemaphoreType.DMA((RING, 10)),
+            pltpu.SemaphoreType.DMA((2,)),
+        ],
+        compiler_params=pltpu.CompilerParams(vmem_limit_bytes=63 * 2**20),
+    )(sums, *states, *rows)
+    return (output, input_grad, *made)
 
 
 def normed(values):
@@ -256,7 +1230,25 @@
     )
 
 
+def local_small(
+    tokens, time_embed, segment_ids, cotangent,
+    mixing_w, mixing_m, mixing_v, mixing_avg,
+    cond_w, cond_m, cond_v, cond_avg,
+    up_w, up_m, up_v, up_avg,
+    down_w, down_m, down_v, down_avg,
+):
+    x, cot = tokens[0], cotangent[0]
+    lse, scales, turn, feat, thirds, w, lt, dpre, qkv, middle, back, output = forward(
+        segment_ids, time_embed, x, cot, mixing_w, cond_w, up_w, down_w)
+    sums, input_grad = backward(turn, lse, scales, time_embed, feat, thirds, w, lt, cot, dpre, qkv, middle, back, x)
+    states = (
+        mixing_w, mixing_m, mixing_v, mixing_avg, cond_w, cond_m, cond_v, cond_avg,
+        up_w, up_m, up_v, up_avg, down_w, down_m, down_v, down_avg)
+    return update(sums, states, (output, input_grad))
+
+
 def solution(mesh):
+    small = mesh.shape["rows"] == 4 and mesh.shape["fsdp"] == 8
     placed = (
         P(("rows", "fsdp"), None, None),
         P(("rows", "fsdp"), None),
@@ -280,7 +1272,7 @@
         P("fsdp", None),
     )
     return jax.shard_map(
-        local,
+        local_small if small else local,
         mesh=mesh,
         in_specs=placed,
         out_specs=(

time: 881 us -> 258 us (0.29); the launches traced: 871 us -> 257 us
  waiting for transfers between devices: 579 us -> 0 us
  Pallas kernels: 0 us -> 256 us
  matrix products: 142 us -> 0 us
  other arithmetic: 81 us -> 0 us
  local copies, waits for them, and re-layouts: 52.8 us -> 0 us
  between operations: 14.8 us -> 0.85 us
    reduce_scatter x4 -> x0, waiting for transfers between devices: 352 us -> none  [the longest x1 117 us: local(): lax.psum_scatter(d_down, 'fsdp', scatter_dimension=0, tiled=True)]
    pallas_call x0 -> x3, Pallas kernels: none -> 256 us  [the longest x1 134 us: backward(): pl.pallas_call(backward_kernel, out_shape=(shape((CHUNKS, 128, 512), BF),...]
    dot_general x19 -> x0, matrix products: 142 us -> none  [the longest x1 15.1 us: local(): jnp.einsum('tf,td->fd', hidden_act, back_out, preferred_element_type=jnp....]
    all_gather x4 -> x0, waiting for transfers between devices: 126 us -> none  [the longest x1 55.4 us: local(): lax.all_gather(mixing_w.astype(jnp.bfloat16), 'fsdp', axis=1, tiled=True)]
    psum x1 -> x0, waiting for transfers between devices: 102 us -> none  [local(): lax.psum(mixing_part.astype(jnp.bfloat16), 'rows').astype(jnp.float32)]
    unnamed x141 -> x0, local copies, waits for them, and re-layouts: 34.8 us -> none
    convert_element_type x12 -> x0, other arithmetic: 27.3 us -> none  [the longest x1 8.23 us: back_block(): (probs_f * (d_probs - jnp.sum(probs_f * d_probs, axis=-1, keepdims=True))...]
    add x6 -> x0, other arithmetic: 24.5 us -> none  [the longest x4 24.4 us: adam_update(): average_new = 0.8 * average + 0.2 * weight_new]
  transfers between devices with their start and end apart: 9 -> 0, of which waited for: 8 -> 0; matrix products, arithmetic and copies ran while one was open for 16% -> 0% of each run, Pallas kernels for 0% -> 0%
where the time goes in v1:
time: 258 us; the launch traced here: 257 us
  Pallas kernels  256 us (99%)
    pallas_call x1, Pallas kernels, backward(): pl.pallas_call(backward_kernel, out_shape=(shape((CHUNKS, 128, 512), BF),...  134 us
    pallas_call x1, Pallas kernels, forward(): pl.pallas_call(forward_kernel, out_shape=(shape((8, 2, 512), F32), shape(...  99.5 us
    pallas_call x1, Pallas kernels, update(): pl.pallas_call(update_kernel, out_shape=tuple(outs), in_specs=[anyw] * 19...  23.2 us

profile of v1, /device:TPU:0, one launch (start us, length us, event | category | flops | bytes accessed | tf_op | source)
XLA Modules:
  0.0 257.3 jit_solution(6728973480474360105)
XLA Ops:
  0.7 99.5 %shard_map.372 = (f32[8,2,512]{2,1,0:T(2,128)}, f32[2,1024]{1,0:T(2,128)}, f32[2,512,128]{2,1,0:T(8,128)}, bf16[2,512,128]{2,1,0:T(8,128)(2,1)}, bf16[3,2,8,128,...) custom-call(s32[1,512]{1,0:T(1,128)} %seg_in.1, ...), custom_call_target="tpu_custom_call" | custom-call | tf_op jit(solution)/shard_map/pallas_call | solution.py:623
  100.1 133.8 %shard_map.373 = (bf16[25,128,512]{2,1,0:T(8,128)(2,1)}, bf16[512,1024]{1,0:T(8,128)(2,1)}) custom-call(f32[2,512,128]{2,1,0:T(8,128)} %get-tuple-element.58.turn_in, f32[8,2,512]{2,1,0:T(2,128)} %get-tuple-element.59.lse_in, f32[2,1024]{1,0:T(2,128)} %get-tuple-element.60.scales_in, bf16[1,256]{1,0:T(2,128)(2,1)} %te_in.3, ...), custom_call_target="tpu_custom_call" | custom-call | tf_op jit(solution)/shard_map/pallas_call | solution.py:835
  234.0 23.2 %shard_map.374 = (f32[4,128,1024]{2,1,0:T(8,128)}, f32[4,128,1024]{2,1,0:T(8,128)}, f32[4,128,1024]{2,1,0:T(8,128)}, f32[4,128,1024]{2,1,0:T(8,128)}, f32[4,128,...) custom-call(bf16[25,128,512]{2,1,0:T(8,128)(2,1)} %get-tuple-element, ...), custom_call_target="tpu_custom_call" | custom-call | tf_op jit(solution)/shard_map/pallas_call | solution.py:967

commit v2 on v1

--- a/solution.py
+++ b/solution.py
@@ -19,13 +19,14 @@
 SLOTS = 4
 SIB_SLOTS = 6
 LINE_SLOTS = 6
-LAGS = (1, 3, 5, 7, 9, 11)
+PART_SLOTS = 10
+LAGS = (1, 3, 5, 7, 9, 11, 13)
 
 
 class Reducer:
     def __init__(self, refs):
-        (self.away, self.part, self.sib, self.diag, self.near, self.zin, self.zmid, self.tsum, self.out_a, self.out_b,
-         self.sems_sib, self.sems_diag, self.sems_near, self.sems_zin, self.sems_zmid) = refs
+        (self.away, self.part, self.sib, self.swap, self.diag, self.near, self.zin, self.zmid, self.tsum, self.out_a, self.out_b,
+         self.sems_sib, self.sems_swap, self.sems_diag, self.sems_near, self.sems_zin, self.sems_zmid) = refs
         self.me = lax.axis_index("fsdp")
         self.core = lax.rem(self.me, 2)
         self.chip = lax.div(self.me, 2)
@@ -39,6 +40,7 @@
         self.chip_x = ybit * 2 + (1 - xbit)
         self.chip_y = (1 - ybit) * 2 + xbit
         self.chip_d = (1 - ybit) * 2 + (1 - xbit)
+        self.mine = pl.multiple_of(lax.rem(self.row, 2) * 64, 64)
         self.to_sib = {"fsdp": self.chip * 2 + (1 - self.core)}
         self.to_x = {"fsdp": self.chip_x * 2 + self.core}
         self.to_y = {"fsdp": self.chip_y * 2 + self.core}
@@ -49,9 +51,10 @@
         bf = jnp.bfloat16
         dma = pltpu.SemaphoreType.DMA
         return [
+            pltpu.VMEM((SLOTS, 4, 128, 512), bf),
+            pltpu.VMEM((PART_SLOTS, 4, 128, 512), bf),
             pltpu.VMEM((SIB_SLOTS, 4, 128, 512), bf),
-            pltpu.VMEM((s, 4, 128, 512), bf),
-            pltpu.VMEM((SIB_SLOTS, 4, 128, 512), bf),
+            pltpu.VMEM((LINE_SLOTS, 64, 512), bf),
             pltpu.VMEM((s, 128, 512), bf),
             pltpu.VMEM((s, 2, 128, 512), bf),
             pltpu.VMEM((LINE_SLOTS, 128, 512), bf),
@@ -60,6 +63,7 @@
             pltpu.VMEM((LINE_SLOTS, 128, 512), bf),
             pltpu.VMEM((LINE_SLOTS, 128, 512), bf),
             dma((2, SIB_SLOTS)),
+            dma((2, LINE_SLOTS)),
             dma((2, s)),
             dma((2, s)),
             dma((2, LINE_SLOTS)),
@@ -85,22 +89,37 @@
             src_ref=src, dst_ref=dst, send_sem=sems.at[which, slot], recv_sem=sems.at[which + sems.shape[0] // 2, slot],
             device_id=to, device_id_type=MESH)
 
-    def c_sib(self, s):
-        return self.copy(self.away.at[s], self.sib.at[s], self.sems_sib, 0, s, self.to_sib)
-
-    def c_diag(self, s, k):
-        to, half = (self.to_x if k == 0 else self.to_y), pl.ds(64 * k, 64)
-        return self.copy(self.part.at[s, self.chip_d, half], self.diag.at[s, half], self.sems_diag, 0, s, to)
-
-    def c_near(self, s, k):
-        to, chip = (self.to_x, self.chip_x) if k == 0 else (self.to_y, self.chip_y)
-        return self.copy(self.part.at[s, chip], self.near.at[s, k], self.sems_near, 0, s, to)
-
-    def both_diag(self, s):
-        return self.copy(self.part.at[s, self.chip_d], self.diag.at[s], self.sems_diag, 0, s, self.to_x)
-
-    def both_near(self, s):
-        return self.copy(self.part.at[s, pl.ds(0, 2)], self.near.at[s], self.sems_near, 0, s, self.to_x)
+    def c_sib(self, g):
+        n = lax.rem(g, SIB_SLOTS)
+        return self.copy(self.away.at[lax.rem(g, SLOTS)], self.sib.at[n], self.sems_sib, 0, n, self.to_sib)
+
+    def shared(self, g):
+        return jnp.logical_and(lax.rem(g, 3) != 2, g < CHUNKS - 4)
+
+    def by_kind(self, g, stage):
+        pl.when(self.shared(g))(lambda: stage(g, self.mine, 32))
+        pl.when(jnp.logical_not(self.shared(g)))(lambda: stage(g, 0, 64))
+
+    def c_swap(self, g):
+        s = lax.rem(g, LINE_SLOTS)
+        theirs = pl.ds(pl.multiple_of(64 - self.mine, 64), 64)
+        return self.copy(self.part.at[lax.rem(g, PART_SLOTS), self.chip_d, theirs], self.swap.at[s], self.sems_swap, 0, s, {"rows": self.line_to})
+
+    def c_diag(self, g, k, first, size):
+        s, to, rows = lax.rem(g, SLOTS), (self.to_x if k == 0 else self.to_y), pl.ds(first + size * k, size)
+        return self.copy(self.part.at[lax.rem(g, PART_SLOTS), self.chip_d, rows], self.diag.at[s, rows], self.sems_diag, 0, s, to)
+
+    def c_near(self, g, k):
+        s, (to, chip) = lax.rem(g, SLOTS), ((self.to_x, self.chip_x) if k == 0 else (self.to_y, self.chip_y))
+        return self.copy(self.part.at[lax.rem(g, PART_SLOTS), chip], self.near.at[s, k], self.sems_near, 0, s, to)
+
+    def both_diag(self, g, first, size):
+        s, rows = lax.rem(g, SLOTS), pl.ds(first, 2 * size)
+        return self.copy(self.part.at[lax.rem(g, PART_SLOTS), self.chip_d, rows], self.diag.at[s, rows], self.sems_diag, 0, s, self.to_x)
+
+    def both_near(self, g):
+        s = lax.rem(g, SLOTS)
+        return self.copy(self.part.at[lax.rem(g, PART_SLOTS), pl.ds(0, 2)], self.near.at[s], self.sems_near, 0, s, self.to_x)
 
     def c_line(self, s):
         return self.copy(self.out_a.at[s], self.zin.at[s], self.sems_zin, 0, s, {"rows": self.line_to})
@@ -108,28 +127,36 @@
     def c_mid(self, s):
         return self.copy(self.out_b.at[s], self.zmid.at[s], self.sems_zmid, 0, s, {"rows": self.mid_to})
 
-    def stage_b(self, g, keep):
+    def stage_b(self, g):
+        p, n = lax.rem(g, PART_SLOTS), lax.rem(g, SIB_SLOTS)
+        self.c_sib(g).wait()
+        self.part[p] = (self.part[p].astype(jnp.float32) + self.sib[n].astype(jnp.float32)).astype(jnp.bfloat16)
+        pl.when(self.shared(g))(lambda: self.c_swap(g).start())
+
+    def add(self, g, chip, first, size, more):
+        p, rows = lax.rem(g, PART_SLOTS), pl.ds(first, size)
+        total = self.part[p, chip, rows].astype(jnp.float32) + more.astype(jnp.float32)
+        self.part[p, chip, rows] = total.astype(jnp.bfloat16)
+
+    def stage_d(self, g, first, size):
+        if size == 32:
+            self.c_swap(g).wait()
+            self.add(g, self.chip_d, first, 64, self.swap[lax.rem(g, LINE_SLOTS)])
+        self.c_diag(g, 0, first, size).start()
+        self.c_diag(g, 1, first, size).start()
+
+    def stage_c(self, g, first, size):
         s = lax.rem(g, SLOTS)
-        n = lax.rem(g, SIB_SLOTS)
-        self.c_sib(n).wait()
-        keep(g, s, n)
-        self.c_diag(s, 0).start()
-        self.c_diag(s, 1).start()
-
-    def stage_c(self, g):
-        s = lax.rem(g, SLOTS)
-        self.both_diag(s).wait()
-        lo = self.part[s, self.chip_y, :64].astype(jnp.float32) + self.diag[s, :64].astype(jnp.float32)
-        self.part[s, self.chip_y, :64] = lo.astype(jnp.bfloat16)
-        self.c_near(s, 1).start()
-        hi = self.part[s, self.chip_x, 64:].astype(jnp.float32) + self.diag[s, 64:].astype(jnp.float32)
-        self.part[s, self.chip_x, 64:] = hi.astype(jnp.bfloat16)
-        self.c_near(s, 0).start()
+        self.both_diag(g, first, size).wait()
+        self.add(g, self.chip_y, first, size, self.diag[s, pl.ds(first, size)])
+        self.c_near(g, 1).start()
+        self.add(g, self.chip_x, first + size, size, self.diag[s, pl.ds(first + size, size)])
+        self.c_near(g, 0).start()
 
     def stage_e(self, g):
-        s = lax.rem(g, SLOTS)
-        self.both_near(s).wait()
-        total = (self.part[s, self.chip].astype(jnp.float32) + self.near[s, 0].astype(jnp.float32)) + self.near[s, 1].astype(jnp.float32)
+        s, p = lax.rem(g, SLOTS), lax.rem(g, PART_SLOTS)
+        self.both_near(g).wait()
+        total = (self.part[p, self.chip].astype(jnp.float32) + self.near[s, 0].astype(jnp.float32)) + self.near[s, 1].astype(jnp.float32)
         n = lax.rem(g, LINE_SLOTS)
         self.tsum[n] = total
 
@@ -170,8 +197,8 @@
         def _():
             self.c_line(s).wait_send()
 
-    def tick(self, t, keep, put):
-        b, c, e, f, h, i = LAGS
+    def tick(self, t, put):
+        b, d, c, e, f, h, i = LAGS
 
         def run(lag, stage, *args):
             g = t - lag
@@ -181,8 +208,9 @@
         run(h, self.stage_h, put)
         run(f, self.stage_f)
         run(e, self.stage_e)
-        run(c, self.stage_c)
-        run(b, self.stage_b, keep)
+        run(c, lambda g: self.by_kind(g, self.stage_c))
+        run(d, lambda g: self.by_kind(g, self.stage_d))
+        run(b, self.stage_b)
 
 
 def dot(a, b):
@@ -695,9 +723,9 @@
 
     def give(g):
         left, right = operands(g)
-        n = lax.rem(g, SIB_SLOTS)
-        red.away[n] = dot(lt[left, 1 - core], right).astype(BF).reshape(4, 128, 512)
-        red.c_sib(n).start()
+        red.away[lax.rem(g, SLOTS)] = dot(lt[left, 1 - core], right).astype(BF).reshape(4, 128, 512)
+        red.part[lax.rem(g, PART_SLOTS)] = dot(lt[left, core], right).astype(BF).reshape(4, 128, 512)
+        red.c_sib(g).start()
 
     def cond_part(parity):
         rows = []
@@ -705,17 +733,6 @@
             column = te_at[2 * chip + parity]
             rows.append(jnp.concatenate([column * dscale[k:k + 1, 512 * h:512 * h + 512] for k in range(2) for h in range(2)], axis=0)[None])
         return jnp.concatenate(rows, axis=0)
-
-    def keep(g, s, n):
-        @pl.when(g < CHUNKS - 1)
-        def _():
-            left, right = operands(g)
-            own = dot(lt[left, core], right).reshape(4, 128, 512)
-            red.part[s] = (own + red.sib[n].astype(F32)).astype(BF)
-
-        @pl.when(g == CHUNKS - 1)
-        def _():
-            red.part[s] = (cond_part(core) + red.sib[n].astype(F32)).astype(BF)
 
     def put(g, value):
         sums[g] = value
@@ -791,9 +808,9 @@
         total = lax.fori_loop(0, 8, norm_one, jnp.zeros((8, 1024), F32), unroll=2)
         dscale[0:1] = jnp.sum(total, axis=0, keepdims=True)
         store_out.start()
-        n = (CHUNKS - 1) % SIB_SLOTS
-        red.away[n] = cond_part(1 - core).astype(BF)
-        red.c_sib(n).start()
+        red.away[(CHUNKS - 1) % SLOTS] = cond_part(1 - core).astype(BF)
+        red.part[(CHUNKS - 1) % PART_SLOTS] = cond_part(core).astype(BF)
+        red.c_sib(jnp.int32(CHUNKS - 1)).start()
 
     store_out = pltpu.make_async_copy(obuf, in_grad, out_sem)
     load_cot.wait()
@@ -817,7 +834,7 @@
         pl.when(jnp.logical_and(m >= 9, m < 12))(lambda: first_back(m - 9))
         pl.when(m == 12)(input_back)
         def ticks(t, carry):
-            red.tick(t, keep, put)
+            red.tick(t, put)
             return carry
 
         lax.fori_loop(2 * m, 2 * m + 2, ticks, 0)

time: 258 us -> 252 us (0.977)
  Pallas kernels: 256 us -> 251 us
    pallas_call x1, Pallas kernels: 134 us -> 129 us  [backward(): pl.pallas_call(backward_kernel, out_shape=(shape((CHUNKS, 128, 512), BF),...]
where the time goes in v2:
time: 252 us
  Pallas kernels  251 us (100%)
    pallas_call x1, Pallas kernels, backward(): pl.pallas_call(backward_kernel, out_shape=(shape((CHUNKS, 128, 512), BF),...  129 us
    pallas_call x1, Pallas kernels, forward(): pl.pallas_call(forward_kernel, out_shape=(shape((8, 2, 512), F32), shape(...  99.5 us
    pallas_call x1, Pallas kernels, update(): pl.pallas_call(update_kernel, out_shape=tuple(outs), in_specs=[anyw] * 19...  23.2 us

profile of v2, /device:TPU:0, one launch (start us, length us, event | category | flops | bytes accessed | tf_op | source)
XLA Modules:
  0.0 252.2 jit_solution(4244524533820673511)
XLA Ops:
  0.7 99.5 %shard_map.372 = (f32[8,2,512]{2,1,0:T(2,128)}, f32[2,1024]{1,0:T(2,128)}, f32[2,512,128]{2,1,0:T(8,128)}, bf16[2,512,128]{2,1,0:T(8,128)(2,1)}, bf16[3,2,8,128,...) custom-call(s32[1,512]{1,0:T(1,128)} %seg_in.1, ...), custom_call_target="tpu_custom_call" | custom-call | tf_op jit(solution)/shard_map/pallas_call | solution.py:651
  100.1 128.7 %shard_map.373 = (bf16[25,128,512]{2,1,0:T(8,128)(2,1)}, bf16[512,1024]{1,0:T(8,128)(2,1)}) custom-call(f32[2,512,128]{2,1,0:T(8,128)} %get-tuple-element.58.turn_in, f32[8,2,512]{2,1,0:T(2,128)} %get-tuple-element.59.lse_in, f32[2,1024]{1,0:T(2,128)} %get-tuple-element.60.scales_in, bf16[1,256]{1,0:T(2,128)(2,1)} %te_in.3, ...), custom_call_target="tpu_custom_call" | custom-call | tf_op jit(solution)/shard_map/pallas_call | solution.py:852
  228.9 23.2 %shard_map.374 = (f32[4,128,1024]{2,1,0:T(8,128)}, f32[4,128,1024]{2,1,0:T(8,128)}, f32[4,128,1024]{2,1,0:T(8,128)}, f32[4,128,1024]{2,1,0:T(8,128)}, f32[4,128,...) custom-call(bf16[25,128,512]{2,1,0:T(8,128)(2,1)} %get-tuple-element, ...), custom_call_target="tpu_custom_call" | custom-call | tf_op jit(solution)/shard_map/pallas_call | solution.py:984

commit v3 on v2

--- a/solution.py
+++ b/solution.py
@@ -94,7 +94,7 @@
         return self.copy(self.away.at[lax.rem(g, SLOTS)], self.sib.at[n], self.sems_sib, 0, n, self.to_sib)
 
     def shared(self, g):
-        return jnp.logical_and(lax.rem(g, 3) != 2, g < CHUNKS - 4)
+        return jnp.logical_and(lax.rem(g, 3) != 2, g < CHUNKS - 2)
 
     def by_kind(self, g, stage):
         pl.when(self.shared(g))(lambda: stage(g, self.mine, 32))
@@ -828,7 +828,6 @@
             give(2 * m)
             give(2 * m + 1)
 
-        pl.when(m == 0)(middle_back)
         pl.when(jnp.logical_and(m >= 1, m < 9))(lambda: attend_back(m - 1))
 
         pl.when(jnp.logical_and(m >= 9, m < 12))(lambda: first_back(m - 9))
@@ -838,6 +837,7 @@
             return carry
 
         lax.fori_loop(2 * m, 2 * m + 2, ticks, 0)
+        pl.when(m == 0)(middle_back)
 
         return carry
 

time: 252 us -> 252 us (level)
  no operation moved by 1% of the time
where the time goes in v3:
time: 252 us
  Pallas kernels  251 us (100%)
    pallas_call x1, Pallas kernels, backward(): pl.pallas_call(backward_kernel, out_shape=(shape((CHUNKS, 128, 512), BF),...  128 us
    pallas_call x1, Pallas kernels, forward(): pl.pallas_call(forward_kernel, out_shape=(shape((8, 2, 512), F32), shape(...  99.5 us
    pallas_call x1, Pallas kernels, update(): pl.pallas_call(update_kernel, out_shape=tuple(outs), in_specs=[anyw] * 19...  23.2 us

profile of v3, /device:TPU:0, one launch (start us, length us, event | category | flops | bytes accessed | tf_op | source)
XLA Modules:
  0.0 251.6 jit_solution(15590575232770075080)
XLA Ops:
  0.7 99.5 %shard_map.372 = (f32[8,2,512]{2,1,0:T(2,128)}, f32[2,1024]{1,0:T(2,128)}, f32[2,512,128]{2,1,0:T(8,128)}, bf16[2,512,128]{2,1,0:T(8,128)(2,1)}, bf16[3,2,8,128,...) custom-call(s32[1,512]{1,0:T(1,128)} %seg_in.1, ...), custom_call_target="tpu_custom_call" | custom-call | tf_op jit(solution)/shard_map/pallas_call | solution.py:651
  100.1 128.1 %shard_map.373 = (bf16[25,128,512]{2,1,0:T(8,128)(2,1)}, bf16[512,1024]{1,0:T(8,128)(2,1)}) custom-call(f32[2,512,128]{2,1,0:T(8,128)} %get-tuple-element.58.turn_in, f32[8,2,512]{2,1,0:T(2,128)} %get-tuple-element.59.lse_in, f32[2,1024]{1,0:T(2,128)} %get-tuple-element.60.scales_in, bf16[1,256]{1,0:T(2,128)(2,1)} %te_in.3, ...), custom_call_target="tpu_custom_call" | custom-call | tf_op jit(solution)/shard_map/pallas_call | solution.py:852
  228.3 23.2 %shard_map.374 = (f32[4,128,1024]{2,1,0:T(8,128)}, f32[4,128,1024]{2,1,0:T(8,128)}, f32[4,128,1024]{2,1,0:T(8,128)}, f32[4,128,1024]{2,1,0:T(8,128)}, f32[4,128,...) custom-call(bf16[25,128,512]{2,1,0:T(8,128)(2,1)} %get-tuple-element, ...), custom_call_target="tpu_custom_call" | custom-call | tf_op jit(solution)/shard_map/pallas_call | solution.py:984

commit v4 on v3

--- a/solution.py
+++ b/solution.py
@@ -723,8 +723,13 @@
 
     def give(g):
         left, right = operands(g)
-        red.away[lax.rem(g, SLOTS)] = dot(lt[left, 1 - core], right).astype(BF).reshape(4, 128, 512)
-        red.part[lax.rem(g, PART_SLOTS)] = dot(lt[left, core], right).astype(BF).reshape(4, 128, 512)
+        halves = dot(lt[left].reshape(1024, 512), right).astype(BF).reshape(2, 4, 128, 512)
+        for p in range(2):
+            @pl.when(core == p)
+            def _(p=p):
+                red.away[lax.rem(g, SLOTS)] = halves[1 - p]
+                red.part[lax.rem(g, PART_SLOTS)] = halves[p]
+
         red.c_sib(g).start()
 
     def cond_part(parity):

time: 252 us -> 252 us (level)
  no operation moved by 1% of the time
where the time goes in v4:
time: 252 us
  Pallas kernels  251 us (100%)
    pallas_call x1, Pallas kernels, backward(): pl.pallas_call(backward_kernel, out_shape=(shape((CHUNKS, 128, 512), BF),...  128 us
    pallas_call x1, Pallas kernels, forward(): pl.pallas_call(forward_kernel, out_shape=(shape((8, 2, 512), F32), shape(...  99.5 us
    pallas_call x1, Pallas kernels, update(): pl.pallas_call(update_kernel, out_shape=tuple(outs), in_specs=[anyw] * 19...  23.2 us

profile of v4, /device:TPU:0, one launch (start us, length us, event | category | flops | bytes accessed | tf_op | source)
XLA Modules:
  0.0 252.0 jit_solution(12984181469558267462)
XLA Ops:
  0.7 99.5 %shard_map.372 = (f32[8,2,512]{2,1,0:T(2,128)}, f32[2,1024]{1,0:T(2,128)}, f32[2,512,128]{2,1,0:T(8,128)}, bf16[2,512,128]{2,1,0:T(8,128)(2,1)}, bf16[3,2,8,128,...) custom-call(s32[1,512]{1,0:T(1,128)} %seg_in.1, ...), custom_call_target="tpu_custom_call" | custom-call | tf_op jit(solution)/shard_map/pallas_call | solution.py:651
  100.1 128.5 %shard_map.373 = (bf16[25,128,512]{2,1,0:T(8,128)(2,1)}, bf16[512,1024]{1,0:T(8,128)(2,1)}) custom-call(f32[2,512,128]{2,1,0:T(8,128)} %get-tuple-element.58.turn_in, f32[8,2,512]{2,1,0:T(2,128)} %get-tuple-element.59.lse_in, f32[2,1024]{1,0:T(2,128)} %get-tuple-element.60.scales_in, bf16[1,256]{1,0:T(2,128)(2,1)} %te_in.3, ...), custom_call_target="tpu_custom_call" | custom-call | tf_op jit(solution)/shard_map/pallas_call | solution.py:857
  228.6 23.2 %shard_map.374 = (f32[4,128,1024]{2,1,0:T(8,128)}, f32[4,128,1024]{2,1,0:T(8,128)}, f32[4,128,1024]{2,1,0:T(8,128)}, f32[4,128,1024]{2,1,0:T(8,128)}, f32[4,128,...) custom-call(bf16[25,128,512]{2,1,0:T(8,128)(2,1)} %get-tuple-element, ...), custom_call_target="tpu_custom_call" | custom-call | tf_op jit(solution)/shard_map/pallas_call | solution.py:989
